TPU v7x, 1024 devices: a whole 4x8x16 slice. The times are simulated.
1024 devices in a mesh: dp: 64 (over x, z), tensor: 16 (over y, core).
Axes of the slice: x: 4, y: 8, z: 16, core: 2. Of those that a mesh axis runs over, the one named last changes fastest.
Arguments:
- residual: bfloat16 [65536, 4096], P(('dp', 'tensor')), may hold values from -6 to 6
- expert_hidden: bfloat16 [1024, 256, 768], P(('dp', 'tensor')), may hold values from -6 to 6
- down_weight: bfloat16 [16, 768, 4096], P('tensor'), may hold values from -0.21875 to 0.21875
- gates: float32 [65536, 2], P(('dp', 'tensor')), may hold values from 0.1 to 0.9
- routes: int32 [65536, 2], P(('dp', 'tensor')), may hold values from 0 to 15, all different within a row; in each aligned block of 64 rows (0 to 63, 64 to 127, ...) at most 16 rows name the same one
- router_probs: float32 [65536, 16], P(('dp', 'tensor')), may hold values from 0 to 14
- norm_gain: float32 [4096], replicated, may hold values from 0.5 to 1.5
- qkv_weight: bfloat16 [4096, 5120], P(None, 'tensor'), may hold values from -0.09375 to 0.09375
Outputs:
- new_residual: bfloat16 [65536, 4096], P(('dp', 'tensor'))
- qkv: bfloat16 [65536, 5120], P('dp', 'tensor')
- balance: float32 [], replicated
Inputs may be any that keep to these rules, and one draw needn't show every extreme that they name: `routes`: within the rows of one device (aligned blocks of 64 tokens) a token names 2 different experts and no expert is named by more than 16 tokens; some expert is named by exactly 16 in some blocks.
All inputs are finite; a program needn't handle non-finite values.
Results may differ from a plain program's by a relative error of at most 0.006.
Values may be sent and summed in bfloat16 or wider, within the bound.
No kernel may reach another device: no remote copies, remote signals or barrier semaphores. Data moves between devices by JAX's collectives and lax.ppermute only.
A program may use at most 64 MiB of HBM per device.

v0:
```python
import jax
import jax.numpy as jnp
from jax import lax
from jax.sharding import PartitionSpec as P

eps = 1e-06


def normalize(rows, norm_gain):
    values = rows.astype(jnp.float32)
    scale = lax.rsqrt(jnp.mean(values * values, axis=-1, keepdims=True) + eps)
    return (values * scale * norm_gain).astype(jnp.bfloat16)


def on_device(
    residual, expert_hidden, down_weight, gates, routes, router_probs, norm_gain, qkv_weight
):
    experts = lax.axis_size("tensor")
    rows_dev, width = residual.shape
    top_count = routes.shape[1]
    slot_count = expert_hidden.shape[1] // experts
    expert_out = jnp.dot(
        expert_hidden[0], down_weight[0], preferred_element_type=jnp.float32
    ).astype(jnp.bfloat16)
    flat_routes = routes.reshape(rows_dev * top_count)
    labels = jnp.arange(experts, dtype=jnp.int32)
    onehot = (flat_routes[:, None] == labels[None, :]).astype(jnp.int32)
    before = jnp.cumsum(onehot, axis=0) - onehot
    slot_rank = jnp.sum(before * onehot, axis=1)
    row_index = flat_routes * slot_count + slot_rank
    returned = lax.all_to_all(
        expert_out.reshape(experts, slot_count, width),
        "tensor",
        split_axis=0,
        concat_axis=0,
        tiled=True,
    )
    columns = returned.shape[2]
    flattened = returned.reshape(experts * slot_count, columns)
    picked = (
        jnp.take(flattened, row_index, axis=0)
        .astype(jnp.float32)
        .reshape(rows_dev, top_count, columns)
    )
    mixture = jnp.sum(gates[:, :, None] * picked, axis=1)
    fresh = (residual.astype(jnp.float32) + mixture).astype(jnp.bfloat16)
    normed = normalize(fresh, norm_gain)
    projected = jnp.dot(
        lax.all_gather(normed, "tensor", axis=0, tiled=True),
        qkv_weight,
        preferred_element_type=jnp.float32,
    ).astype(jnp.bfloat16)
    counts = jnp.sum(onehot, axis=0).astype(jnp.float32)
    shares = jnp.sum(router_probs, axis=0)
    totals = lax.psum((counts, shares), ("dp", "tensor"))
    total_tokens = rows_dev * lax.axis_size("dp") * experts
    usage = totals[0] / (total_tokens * top_count)
    share_mean = totals[1] / total_tokens
    balance = experts * jnp.sum(usage * share_mean)
    return (fresh, projected, balance)


def solution(mesh):
    in_specs = (
        P(("dp", "tensor"), None),
        P(("dp", "tensor"), None, None),
        P("tensor", None, None),
        P(("dp", "tensor"), None),
        P(("dp", "tensor"), None),
        P(("dp", "tensor"), None),
        P(),
        P(None, "tensor"),
    )
    out_specs = (P(("dp", "tensor"), None), P("dp", "tensor"), P())
    return jax.shard_map(
        on_device, mesh=mesh, in_specs=in_specs, out_specs=out_specs, check_vma=False
    )
```

profile of v0, /device:TPU:1, one launch (start us, length us, event | category | flops | bytes accessed | tf_op | source)
XLA Modules:
  0.0 238.1 jit_solution(16357543848120164771)
XLA Ops:
  7.2 0.0 copy-start
  7.2 6.1 %fusion.2 = bf16[256,4096]{1,0:T(8,128)(2,1)} fusion(bf16[1,768,4096]{2,1,0:T(8,128)(2,1)} %param.10, bf16[1,256,768]{2,1,0:T(8,128)(2,1)} %param.9), kind=kOutput, calls=%fused_computation.3 | convolution fusion | flops 1611661312 | bytes 8781824 | tf_op jit(solution)/shard_map/dot_general | solution.py:22
  13.3 18.4 %all-to-all-start = ((bf16[16,16,4096]{2,1,0:T(8,128)(2,1)}), bf16[16,16,4096]{2,1,0:T(8,128)(2,1)}, u32[]{:S(2)}, u32[]{:S(2)}) async-start(bf16[16,16,4096]{2,1,0:T(8,128)(2,1)} %bitcast.18), calls=%async_computation | async-start | bytes 4194304 | tf_op jit(solution)/shard_map/all_to_all | solution.py:31
  31.8 0.0 all-gather.2.cloned.1.call-start
  31.8 0.0 copy-done.3
  31.8 0.1 copy.18
  31.9 0.1 copy.21
  32.0 0.1 mul.56
  32.2 0.0 copy-done.5
  32.2 0.1 copy.17
  32.3 0.1 reshape.68
  32.4 0.1 fusion.9
  32.5 0.2 reduce_window_sum.11
  32.7 0.2 fusion.10
  32.9 0.1 reduce_sum.59
  33.0 0.1 copy.19
  33.1 0.1 copy.20
  33.2 47.6 %all-to-all-done = bf16[16,16,4096]{2,1,0:T(8,128)(2,1)} async-done(((bf16[16,16,4096]{2,1,0:T(8,128)(2,1)}), bf16[16,16,4096]{2,1,0:T(8,128)(2,1)}, u32[]{:S(2)}, u32[]{:S(2)}) %all-to-all-start) | async-done | bytes 2097184 | tf_op jit(solution)/shard_map/all_to_all | solution.py:31
  80.9 5.0 %gather_fusion = bf16[128,4096]{1,0:T(8,128)(2,1)} fusion(bf16[256,4096]{1,0:T(8,128)(2,1)} %bitcast.3, s32[1024]{0:T(1024)S(1)} %pad_clamp_fusion), kind=kCustom, calls=%fused_computation | custom fusion | bytes 2097664 | tf_op jit(solution)/shard_map/jit(_take)/gather | solution.py:41
  85.9 2.5 %gather.7 = bf16[64,2,4096]{2,1,0:T(2,128)(2,1)} reshape(bf16[128,4096]{1,0:T(8,128)(2,1)} %gather_fusion) | data formatting | bytes 2097152 | tf_op jit(solution)/shard_map/jit(_take)/gather | solution.py:41
  88.4 5.5 %multiply_reduce_fusion = f32[64,4096]{1,0:T(8,128)S(1)} fusion(bf16[64,2,4096]{2,1,0:T(2,128)(2,1)} %gather.7, pred[64,2]{1,0:T(8,128)(4,1)S(1)} %copy.20, f32[64,2]{1,0:T(8,128)S(1)} %copy.17), kind=kLoop, calls=%fused_computation.4 | loop fusion | flops 1835008 | bytes 2097792 | tf_op jit(solution)/shard_map/reduce_sum | solution.py:45
  94.0 1.3 fusion.5
  95.3 0.0 copy-start.1
  95.3 0.0 copy-done.2
  95.3 1.0 fusion.7
  96.3 0.0 all-gather.2.cloned.1.call-update
  96.3 0.0 copy-done.4
  96.4 0.1 reduce_sum.64
  96.5 125.2 %all-reduce = (f32[16]{0:T(128)S(1)}, f32[16]{0:T(128)S(1)}) all-reduce(f32[16]{0:T(128)S(1)} %reduce_sum.64, f32[16]{0:T(128)S(1)} %convert_element_type.36), channel_id=1, replica_groups=mesh['dp'=64,'tensor'=16] {'dp','tensor'}, use_global_device_ids=true, to_apply=%region_7.8 | all-reduce | flops 32 | bytes 256 | tf_op jit(solution)/shard_map/psum | solution.py:55
  221.7 0.6 multiply_reduce_fusion.1
  222.9 0.0 all-gather.2.cloned.1.call-done
  223.0 7.1 %convolution_convert_fusion = bf16[1024,320]{0,1:T(8,128)(2,1)} fusion(bf16[1024,4096]{1,0:T(8,128)(2,1)} %all-gather.2.cloned.1.call-done, bf16[4096,320]{0,1:T(8,128)(2,1)S(1)} %copy-done), kind=kOutput, calls=%fused_computation.6 | convolution fusion | flops 2684682240 | bytes 11665408 | tf_op jit(solution)/shard_map/dot_general | solution.py:48
  (12 shorter events, 0.0 us)
Async XLA Ops:
  7.2 215.8 %copy-start = (bf16[4096,320]{0,1:T(8,128)(2,1)S(1)}, bf16[4096,320]{0,1:T(8,128)(2,1)}, u32[]{:S(2)}) copy-start(bf16[4096,320]{0,1:T(8,128)(2,1)} %param.15) | copy-start | bytes 7864324
  13.3 18.5 %copy-start.3 = (s32[64,2]{0,1:T(2,128)S(1)}, s32[64,2]{0,1:T(2,128)}, u32[]{:S(2)}) copy-start(s32[64,2]{0,1:T(2,128)} %param.12) | copy-start | bytes 1540
  13.3 18.8 %copy-start.5 = (f32[64,2]{0,1:T(2,128)S(1)}, f32[64,2]{0,1:T(2,128)}, u32[]{:S(2)}) copy-start(f32[64,2]{0,1:T(2,128)} %param.11) | copy-start | bytes 1540
  13.3 67.5 %all-to-all-start = ((bf16[16,16,4096]{2,1,0:T(8,128)(2,1)}), bf16[16,16,4096]{2,1,0:T(8,128)(2,1)}, u32[]{:S(2)}, u32[]{:S(2)}) async-start(bf16[16,16,4096]{2,1,0:T(8,128)(2,1)} %bitcast.18), calls=%async_computation | async-start | bytes 4194304 | tf_op jit(solution)/shard_map/all_to_all | solution.py:31
  31.8 191.2 %all-gather.2.cloned.1.call-start = ((), (), s32[]{:S(2)}) async-start(), calls=%async_computation.1 | async-start | bytes 8912896 | tf_op jit(solution)/shard_map/all_gather | solution.py:49
  88.4 6.9 %copy-start.2 = (f32[4096]{0:T(1024)S(1)}, f32[4096]{0:T(1024)}, u32[]{:S(2)}) copy-start(f32[4096]{0:T(1024)} %param.14) | copy-start | bytes 49156
  88.4 7.9 %copy-start.4 = (f32[64,16]{0,1:T(8,128)S(1)}, f32[64,16]{0,1:T(8,128)}, u32[]{:S(2)}) copy-start(f32[64,16]{0,1:T(8,128)} %param.13) | copy-start | bytes 12292
  95.3 134.8 %copy-start.1 = (bf16[64,4096]{1,0:T(8,128)(2,1)}, bf16[64,4096]{1,0:T(8,128)(2,1)S(1)}, u32[]{:S(2)}) copy-start(bf16[64,4096]{1,0:T(8,128)(2,1)S(1)} %get-tuple-element.8) | copy-start | bytes 1572868
Sparse Core Ops, SparseCore 0:
  96.5 59.7 all-gather.1
where the time goes:
time: 238 us
  blocking collectives  125 us (53%)
  waiting for transfers between devices  47.7 us (20%)
  starting transfers between devices  18.5 us (8%)
  between operations  16 us (7%)
  matrix products  13.3 us (6%)
  other arithmetic  9.01 us (4%)
  local copies, waits for them, and re-layouts  8.51 us (4%)
    psum x1, blocking collectives, on_device(): totals = lax.psum((counts, shares), ('dp', 'tensor'))  125 us
    all_to_all x1, waiting for transfers between devices, on_device(): lax.all_to_all(expert_out.reshape(experts, slot_count, width), 'tensor',...  47.6 us
    all_to_all x1, starting transfers between devices, on_device(): lax.all_to_all(expert_out.reshape(experts, slot_count, width), 'tensor',...  18.4 us
    gather x2, local copies, waits for them, and re-layouts, on_device(): jnp.take(flattened, row_index, axis=0).astype(jnp.float32)  7.59 us
    dot_general x1, matrix products, on_device(): jnp.dot(lax.all_gather(normed, 'tensor', axis=0, tiled=True), qkv_weight,...  7.12 us
    dot_general x1, matrix products, on_device(): jnp.dot(expert_hidden[0], down_weight[0], preferred_element_type=jnp.floa...  6.15 us
    reduce_sum x1, other arithmetic, on_device(): mixture = jnp.sum(gates[:, :, None] * picked, axis=1)  5.52 us
  transfers between devices with their start and end apart: 2, of which 1 were waited for; matrix products, arithmetic and copies ran while one was open for 1% of the time, Pallas kernels for 0%

commit v1 on v0

v1 whole, which is shorter than its diff:
```python
import jax
import jax.numpy as jnp
from jax import lax
from jax.experimental import pallas as pl
from jax.experimental.pallas import tpu as pltpu
from jax.sharding import PartitionSpec as P

eps = 1e-06


def expert_kernel(hidden_ref, weight_ref, routes_ref, probs_ref, out_ref, counts_ref, shares_ref):
    out_ref[...] = jnp.dot(
        hidden_ref[...], weight_ref[...], preferred_element_type=jnp.float32
    ).astype(jnp.bfloat16)

    @pl.when(pl.program_id(0) == 0)
    def _():
        routes = routes_ref[...]
        rows, experts = probs_ref.shape
        label = lax.broadcasted_iota(jnp.int32, (rows, experts), 1)
        named = jnp.where(label == routes[:, 0:1], 1.0, 0.0)
        for j in range(1, routes.shape[1]):
            named = named + jnp.where(label == routes[:, j : j + 1], 1.0, 0.0)
        counts_ref[...] = jnp.sum(named, axis=0, keepdims=True)
        shares_ref[...] = jnp.sum(probs_ref[...], axis=0, keepdims=True)


def expert_project(hidden, weight, routes, probs, steps=4):
    slots, depth = hidden.shape
    width = weight.shape[1]
    block = width // steps
    whole = lambda shape: pl.BlockSpec(shape, lambda i: (0, 0))
    return pl.pallas_call(
        expert_kernel,
        grid=(steps,),
        in_specs=[
            whole(hidden.shape),
            pl.BlockSpec((depth, block), lambda i: (0, i)),
            whole(routes.shape),
            whole(probs.shape),
        ],
        out_specs=[
            pl.BlockSpec((slots, block), lambda i: (0, i)),
            whole((1, probs.shape[1])),
            whole((1, probs.shape[1])),
        ],
        out_shape=[
            jax.ShapeDtypeStruct((slots, width), jnp.bfloat16),
            jax.ShapeDtypeStruct((1, probs.shape[1]), jnp.float32),
            jax.ShapeDtypeStruct((1, probs.shape[1]), jnp.float32),
        ],
        compiler_params=pltpu.CompilerParams(vmem_limit_bytes=56 * 2**20),
        cost_estimate=pl.CostEstimate(
            flops=2 * slots * depth * width,
            bytes_accessed=2 * (depth * width + slots * (depth + width)),
            transcendentals=0,
        ),
        name="expert_project",
    )(hidden, weight, routes, probs)


def pick_kernel(slot_count, routes_ref, gates_ref, high_ref, low_ref):
    rows, columns = high_ref.shape
    lane = lax.broadcasted_iota(jnp.int32, (rows, columns), 1)
    expert = lax.shift_right_logical(lane, slot_count.bit_length() - 1)
    slot = (lane & (slot_count - 1)).astype(jnp.float32)
    named = jnp.zeros((rows, columns), jnp.float32)
    gate = jnp.zeros((rows, columns), jnp.float32)
    for j in range(routes_ref.shape[1]):
        hit = expert == routes_ref[:, j : j + 1]
        named = named + jnp.where(hit, 1.0, 0.0)
        gate = gate + jnp.where(hit, gates_ref[:, j : j + 1], 0.0)
    row = lax.broadcasted_iota(jnp.int32, (rows, rows), 0)
    column = lax.broadcasted_iota(jnp.int32, (rows, rows), 1)
    earlier = jnp.where(column < row, 1.0, 0.0).astype(jnp.bfloat16)
    rank = jnp.dot(earlier, named.astype(jnp.bfloat16), preferred_element_type=jnp.float32)
    pick = jnp.where(rank == slot, gate, 0.0)
    high = pick.astype(jnp.bfloat16)
    high_ref[...] = high
    low_ref[...] = (pick - high.astype(jnp.float32)).astype(jnp.bfloat16)


def pick_matrix(routes, gates, columns, slot_count):
    rows = routes.shape[0]
    shape = jax.ShapeDtypeStruct((rows, columns), jnp.bfloat16)
    return pl.pallas_call(
        lambda *refs: pick_kernel(slot_count, *refs),
        out_shape=[shape, shape],
        name="pick_matrix",
    )(routes, gates)


def combine_kernel(
    high_ref,
    low_ref,
    slots_ref,
    residual_ref,
    gain_ref,
    counts_ref,
    shares_ref,
    fresh_ref,
    normed_ref,
    counts_out_ref,
    shares_out_ref,
):
    rows, width = residual_ref.shape
    counts_out_ref[...] = counts_ref[...]
    shares_out_ref[...] = shares_ref[...]
    pick = jnp.concatenate([high_ref[...], low_ref[...]], axis=0)
    block = 512
    total = jnp.zeros((rows, 128), jnp.float32)
    for start in range(0, width, block):
        at = pl.ds(start, block)
        both = jnp.dot(pick, slots_ref[:, at], preferred_element_type=jnp.float32)
        mixture = both[:rows] + both[rows:]
        fresh = (residual_ref[:, at].astype(jnp.float32) + mixture).astype(jnp.bfloat16)
        fresh_ref[:, at] = fresh
        values = fresh.astype(jnp.float32)
        square = values * values
        for lane in range(0, block, 128):
            total = total + square[:, lane : lane + 128]
    mean = jnp.sum(total, axis=1, keepdims=True) / width
    scale = lax.rsqrt(mean + eps)
    for start in range(0, width, block):
        at = pl.ds(start, block)
        values = fresh_ref[:, at].astype(jnp.float32)
        normed_ref[:, at] = (values * scale * gain_ref[:, at]).astype(jnp.bfloat16)


def combine(high, low, slots, residual, gain, counts, shares):
    rows, width = residual.shape
    return pl.pallas_call(
        combine_kernel,
        out_shape=[
            jax.ShapeDtypeStruct((rows, width), jnp.bfloat16),
            jax.ShapeDtypeStruct((rows, width), jnp.bfloat16),
            jax.ShapeDtypeStruct(counts.shape, jnp.float32),
            jax.ShapeDtypeStruct(shares.shape, jnp.float32),
        ],
        compiler_params=pltpu.CompilerParams(vmem_limit_bytes=16 * 2**20),
        cost_estimate=pl.CostEstimate(
            flops=4 * rows * slots.shape[0] * width,
            bytes_accessed=2 * (slots.size + 3 * residual.size),
            transcendentals=0,
        ),
        name="combine_and_norm",
    )(high, low, slots, residual, gain, counts, shares)


def project_kernel(weight_ref, rows_ref, out_ref):
    out_ref[...] = lax.dot_general(
        weight_ref[...],
        rows_ref[...],
        (((1,), (1,)), ((), ())),
        preferred_element_type=jnp.float32,
    ).astype(jnp.bfloat16)


def project(rows, weight_t, block=256):
    count, width = rows.shape
    columns = weight_t.shape[0]
    return pl.pallas_call(
        project_kernel,
        grid=(count // block,),
        in_specs=[
            pl.BlockSpec((columns, width), lambda i: (0, 0)),
            pl.BlockSpec((block, width), lambda i: (i, 0)),
        ],
        out_specs=pl.BlockSpec((columns, block), lambda i: (0, i)),
        out_shape=jax.ShapeDtypeStruct((columns, count), jnp.bfloat16),
        compiler_params=pltpu.CompilerParams(vmem_limit_bytes=56 * 2**20),
        cost_estimate=pl.CostEstimate(
            flops=2 * count * width * columns,
            bytes_accessed=2 * (count * width + columns * (width + count)),
            transcendentals=0,
        ),
        name="qkv_project",
    )(weight_t, rows)


def on_device(
    residual, expert_hidden, down_weight, gates, routes, router_probs, norm_gain, qkv_weight
):
    experts = lax.axis_size("tensor")
    rows_dev, width = residual.shape
    top_count = routes.shape[1]
    slot_count = expert_hidden.shape[1] // experts
    expert_out, counts, shares = expert_project(
        expert_hidden[0], down_weight[0], routes, router_probs
    )
    returned = lax.all_to_all(
        expert_out.reshape(experts, slot_count, width),
        "tensor",
        split_axis=0,
        concat_axis=0,
        tiled=True,
    ).reshape(experts * slot_count, width)
    depth = 16
    breadth = lax.axis_size("dp") // depth
    lines = [[x * depth + z for z in range(depth)] for x in range(breadth)]
    cross = [[x * depth + z for x in range(breadth)] for z in range(depth)]
    sums = lax.psum((counts, shares), "dp", axis_index_groups=cross)
    sums = lax.psum(sums, "dp", axis_index_groups=lines)
    high, low = pick_matrix(routes, gates, experts * slot_count, slot_count)
    fresh, normed, counts, shares = combine(
        high, low, returned, residual, norm_gain.reshape(1, width), *sums
    )
    gathered = lax.all_gather(normed, "tensor", axis=0, tiled=True)
    totals = lax.psum((counts, shares), "tensor")
    total_tokens = rows_dev * lax.axis_size("dp") * experts
    usage = totals[0] / (total_tokens * top_count)
    share_mean = totals[1] / total_tokens
    balance = experts * jnp.sum(usage * share_mean)
    projected = project(gathered, qkv_weight.T).T
    return (fresh, projected, balance)


def solution(mesh):
    in_specs = (
        P(("dp", "tensor"), None),
        P(("dp", "tensor"), None, None),
        P("tensor", None, None),
        P(("dp", "tensor"), None),
        P(("dp", "tensor"), None),
        P(("dp", "tensor"), None),
        P(),
        P(None, "tensor"),
    )
    out_specs = (P(("dp", "tensor"), None), P("dp", "tensor"), P())
    return jax.shard_map(
        on_device, mesh=mesh, in_specs=in_specs, out_specs=out_specs, check_vma=False
    )
```

time: 238 us -> 162 us (0.68)
  blocking collectives: 125 us -> 61.9 us
  Pallas kernels: 0 us -> 16.6 us
  matrix products: 13.3 us -> 0 us
  other arithmetic: 9.01 us -> 0.6 us
  waiting for transfers between devices: 47.7 us -> 43.6 us
  local copies, waits for them, and re-layouts: 8.51 us -> 5.03 us
    psum x1 -> x3, blocking collectives: 125 us -> 61.9 us  [the longest x1 31.9 us: on_device(): sums = lax.psum(sums, 'dp', axis_index_groups=lines)]
    all_to_all x1, waiting for transfers between devices: 47.6 us -> 8.1 us  [on_device(): lax.all_to_all(expert_out.reshape(experts, slot_count, width), 'tensor',...]
    all_gather x1, waiting for transfers between devices: 0.02 us -> 35.5 us  [on_device(): gathered = lax.all_gather(normed, 'tensor', axis=0, tiled=True)]
    pallas_call x0 -> x4, Pallas kernels: none -> 16.6 us  [the longest x1 7.5 us: project(): pl.pallas_call(project_kernel, grid=(count // block,), in_specs=[pl.Block...]
    dot_general x2 -> x0, matrix products: 13.3 us -> none  [the longest x1 7.12 us: on_device(): jnp.dot(lax.all_gather(normed, 'tensor', axis=0, tiled=True), qkv_weight,...]
    gather x2 -> x0, local copies, waits for them, and re-layouts: 7.59 us -> none  [on_device(): jnp.take(flattened, row_index, axis=0).astype(jnp.float32)]
    reduce_sum x4 -> x0, other arithmetic: 7.13 us -> none  [the longest x1 5.52 us: on_device(): mixture = jnp.sum(gates[:, :, None] * picked, axis=1)]
    unnamed x14 -> x17, local copies, waits for them, and re-layouts: 0.22 us -> 5.03 us
  transfers between devices with their start and end apart: 2 -> 2, of which waited for: 1 -> 2; matrix products, arithmetic and copies ran while one was open for 1% -> 1% of each run, Pallas kernels for 0% -> 1%
where the time goes in v1:
time: 162 us; the launch traced here: 161 us
  blocking collectives  61.9 us (38%)
  waiting for transfers between devices  43.6 us (27%)
  starting transfers between devices  17.8 us (11%)
  Pallas kernels  16.6 us (10%)
  between operations  15.8 us (10%)
  local copies, waits for them, and re-layouts  5.03 us (3%)
    all_gather x1, waiting for transfers between devices, on_device(): gathered = lax.all_gather(normed, 'tensor', axis=0, tiled=True)  35.5 us
    psum x1, blocking collectives, on_device(): sums = lax.psum(sums, 'dp', axis_index_groups=lines)  31.9 us
    psum x1, blocking collectives, on_device(): totals = lax.psum((counts, shares), 'tensor')  23.4 us
    all_to_all x1, starting transfers between devices, on_device(): lax.all_to_all(expert_out.reshape(experts, slot_count, width), 'tensor',...  17.8 us
    all_to_all x1, waiting for transfers between devices, on_device(): lax.all_to_all(expert_out.reshape(experts, slot_count, width), 'tensor',...  8.1 us
    pallas_call x1, Pallas kernels, project(): pl.pallas_call(project_kernel, grid=(count // block,), in_specs=[pl.Block...  7.5 us
    psum x1, blocking collectives, on_device(): sums = lax.psum((counts, shares), 'dp', axis_index_groups=cross)  6.59 us
    pallas_call x1, Pallas kernels, expert_project(): pl.pallas_call(expert_kernel, grid=(steps,), in_specs=[whole(hidden.shape...  5.96 us
  transfers between devices with their start and end apart: 2, of which 2 were waited for; matrix products, arithmetic and copies ran while one was open for 1% of the time, Pallas kernels for 1%

profile of v1, /device:TPU:1, one launch (start us, length us, event | category | flops | bytes accessed | tf_op | source)
XLA Modules:
  0.0 161.3 jit_solution(6464463760365859005)
XLA Ops:
  7.2 1.4 copy.11.refs_0_.routes_ref
  8.5 1.4 copy.14.probs_ref
  9.9 6.0 %expert_project.1 = (bf16[256,4096]{1,0:T(8,128)(2,1)}, f32[1,16]{1,0:T(1,128)}, f32[1,16]{1,0:T(1,128)}) custom-call(bf16[256,768]{1,0:T(8,128)(2,1)} %bitcast.13, bf16[768,4096]{1,0:T(8,128)(2,1)} %bitcast.9, s32[64,2]{1,0:T(8,128)} %copy.11.refs_0_.routes_ref, f32[64,16]{1,0:T(8,128)} %copy.14.probs_ref), custom_call_target="tpu_custom_call" | custom-call | flops 1610612736 | bytes 8781824 | tf_op jit(solution)/shard_map/expert_project/pallas_call | solution.py:33
  15.9 0.0 copy-start.4
  15.9 0.0 copy-start.5
  15.9 0.0 copy-start.6
  15.9 0.0 copy-start
  15.9 0.0 copy-start.3
  15.9 17.8 %all-to-all-start = ((bf16[16,16,4096]{2,1,0:T(8,128)(2,1)}), bf16[16,16,4096]{2,1,0:T(8,128)(2,1)S(1)}, u32[]{:S(2)}, u32[]{:S(2)}) async-start(bf16[16,16,4096]{2,1,0:T(8,128)(2,1)} %bitcast.11), calls=%async_computation | async-start | bytes 4194304 | tf_op jit(solution)/shard_map/all_to_all | solution.py:191
  33.7 0.0 all-gather.2.cloned.1.call-start
  33.8 0.0 copy-done.4
  33.8 0.7 copy.12.refs_1_
  34.5 1.6 %pick_matrix.1 = (bf16[64,256]{1,0:T(8,128)(2,1)}, bf16[64,256]{1,0:T(8,128)(2,1)}) custom-call(s32[64,2]{1,0:T(8,128)} %copy.11.refs_0_.routes_ref, f32[64,2]{1,0:T(8,128)} %copy.12.refs_1_), custom_call_target="tpu_custom_call" | custom-call | tf_op jit(solution)/shard_map/pick_matrix/pallas_call | solution.py:86
  36.1 0.0 copy-done.5
  36.1 0.0 copy-done.6
  36.1 6.6 %all-reduce.2 = (f32[1,16]{1,0:T(1,128)S(1)}, f32[1,16]{1,0:T(1,128)S(1)}) all-reduce(f32[1,16]{1,0:T(1,128)S(1)} %copy-done.5, f32[1,16]{1,0:T(1,128)S(1)} %copy-done.6), channel_id=1, replica_groups={{0,256,512,768},{16,272,528,784},{32,288,544,800},{48,304,560,816},{64,..., use_global_device_ids=true, to_apply=%region_0.0 | all-reduce | flops 32 | bytes 256 | tf_op jit(solution)/shard_map/psum | solution.py:202
  42.7 31.9 %all-reduce.1 = (f32[1,16]{1,0:T(1,128)S(1)}, f32[1,16]{1,0:T(1,128)S(1)}) all-reduce(f32[1,16]{1,0:T(1,128)S(1)} %get-tuple-element.25, f32[1,16]{1,0:T(1,128)S(1)} %get-tuple-element.26), channel_id=1, replica_groups={{0,16,32,48,64,80,96,112,128,144,160,176,192,208,224,240},{256,272,288,..., use_global_device_ids=true, to_apply=%region_1.0 | all-reduce | flops 32 | bytes 256 | tf_op jit(solution)/shard_map/psum | solution.py:203
  74.6 8.1 %all-to-all-done = bf16[16,16,4096]{2,1,0:T(8,128)(2,1)S(1)} async-done(((bf16[16,16,4096]{2,1,0:T(8,128)(2,1)}), bf16[16,16,4096]{2,1,0:T(8,128)(2,1)S(1)}, u32[]{:S(2)}, u32[]{:S(2)}) %all-to-all-start) | async-done | bytes 2097184 | tf_op jit(solution)/shard_map/all_to_all | solution.py:191
  82.7 0.0 copy-done
  82.7 0.0 copy-done.3
  82.7 0.0 copy-start.1
  82.7 0.8 copy-done.1
  83.5 0.0 copy-start.2
  83.5 0.8 copy-done.2
  84.2 1.5 combine_and_norm.1
  85.7 0.0 all-gather.2.cloned.1.call-update
  85.8 23.4 %all-reduce = (f32[1,16]{1,0:T(1,128)S(1)}, f32[1,16]{1,0:T(1,128)S(1)}) all-reduce(f32[1,16]{1,0:T(1,128)S(1)} %get-tuple-element.20, f32[1,16]{1,0:T(1,128)S(1)} %get-tuple-element.19), channel_id=1, replica_groups=mesh['dp'=64,'tensor'=16] {'tensor'}, use_global_device_ids=true, to_apply=%region_5.0 | all-reduce | flops 32 | bytes 256 | tf_op jit(solution)/shard_map/psum | solution.py:209
  109.1 0.6 multiply_reduce_fusion
  110.4 35.5 %all-gather.2.cloned.1.call-done.rows_ref = bf16[1024,4096]{1,0:T(8,128)(2,1)} async-done(((bf16[64,4096]{1,0:T(8,128)(2,1)}), bf16[1024,4096]{1,0:T(8,128)(2,1)}) %all-gather.2.cloned.1.call-update) | async-done | bytes 8388624 | tf_op jit(solution)/shard_map/all_gather | solution.py:208
  145.9 7.5 %qkv_project.1 = bf16[320,1024]{1,0:T(8,128)(2,1)} custom-call(bf16[320,4096]{1,0:T(8,128)(2,1)} %bitcast.10, bf16[1024,4096]{1,0:T(8,128)(2,1)} %all-gather.2.cloned.1.call-done.rows_ref), custom_call_target="tpu_custom_call" | custom-call | flops 2684354560 | bytes 11665408 | tf_op jit(solution)/shard_map/qkv_project/pallas_call | solution.py:162
Async XLA Ops:
  15.9 17.9 %copy-start.4 = (f32[64,2]{0,1:T(2,128)S(1)}, f32[64,2]{0,1:T(2,128)}, u32[]{:S(2)}) copy-start(f32[64,2]{0,1:T(2,128)} %param.11) | copy-start | bytes 1540
  15.9 20.2 %copy-start.5 = (f32[1,16]{1,0:T(1,128)S(1)}, f32[1,16]{1,0:T(1,128)}, u32[]{:S(2)}) copy-start(f32[1,16]{1,0:T(1,128)} %get-tuple-element.15) | copy-start | bytes 196
  15.9 20.2 %copy-start.6 = (f32[1,16]{1,0:T(1,128)S(1)}, f32[1,16]{1,0:T(1,128)}, u32[]{:S(2)}) copy-start(f32[1,16]{1,0:T(1,128)} %get-tuple-element.16) | copy-start | bytes 196
  15.9 66.8 %copy-start = (bf16[64,4096]{1,0:T(8,128)(2,1)S(1)}, bf16[64,4096]{1,0:T(8,128)(2,1)}, u32[]{:S(2)}) copy-start(bf16[64,4096]{1,0:T(8,128)(2,1)} %residual_ref.1) | copy-start | bytes 1572868
  15.9 66.8 %copy-start.3 = (f32[4096]{0:T(1024)S(1)}, f32[4096]{0:T(1024)}, u32[]{:S(2)}) copy-start(f32[4096]{0:T(1024)} %param.14) | copy-start | bytes 49156
  15.9 66.8 %all-to-all-start = ((bf16[16,16,4096]{2,1,0:T(8,128)(2,1)}), bf16[16,16,4096]{2,1,0:T(8,128)(2,1)S(1)}, u32[]{:S(2)}, u32[]{:S(2)}) async-start(bf16[16,16,4096]{2,1,0:T(8,128)(2,1)} %bitcast.11), calls=%async_computation | async-start | bytes 4194304 | tf_op jit(solution)/shard_map/all_to_all | solution.py:191
  33.7 112.1 %all-gather.2.cloned.1.call-start = ((), (), s32[]{:S(2)}) async-start(), calls=%async_computation.1 | async-start | bytes 8912896 | tf_op jit(solution)/shard_map/all_gather | solution.py:208
  82.7 0.8 copy-start.1
  83.5 0.8 copy-start.2
Sparse Core Ops, SparseCore 0:
  85.9 59.9 all-gather.1

commit v2 on v1

v2 whole, which is shorter than its diff:
```python
import jax
import jax.numpy as jnp
from jax import lax
from jax.experimental import pallas as pl
from jax.experimental.pallas import tpu as pltpu
from jax.sharding import PartitionSpec as P

eps = 1e-06
lanes = 128
MIB = 2**20


def expert_kernel(hidden_ref, *refs):
    weight_refs, out_ref = refs[:-1], refs[-1]
    depth = weight_refs[0].shape[0]
    total = None
    for k, weight_ref in enumerate(weight_refs):
        part = jnp.dot(
            hidden_ref[:, k * depth : (k + 1) * depth],
            weight_ref[...],
            preferred_element_type=jnp.float32,
        )
        total = part if total is None else total + part
    out_ref[...] = total.astype(jnp.bfloat16)


def expert_project(hidden, weight, steps=2, parts=1):
    slots, depth = hidden.shape
    width = weight.shape[1]
    block = width // steps
    weight_spec = lambda k: pl.BlockSpec((depth // parts, block), lambda i: (k, i))
    return pl.pallas_call(
        expert_kernel,
        grid=(steps,),
        in_specs=[pl.BlockSpec((slots, depth), lambda i: (0, 0))]
        + [weight_spec(k) for k in range(parts)],
        out_specs=pl.BlockSpec((slots, block), lambda i: (0, i)),
        out_shape=jax.ShapeDtypeStruct((slots, width), jnp.bfloat16),
        compiler_params=pltpu.CompilerParams(vmem_limit_bytes=56 * MIB),
        cost_estimate=pl.CostEstimate(
            flops=2 * slots * depth * width,
            bytes_accessed=2 * (depth * width + slots * (depth + width)),
            transcendentals=0,
        ),
        name="expert_project",
    )(hidden, *([weight] * parts))


def pick_kernel(slot_count, routes_ref, gates_ref, probs_ref, pick_ref, counts_ref, shares_ref):
    top_count, rows = routes_ref.shape
    experts = probs_ref.shape[0]
    count = experts * slot_count
    place = lax.broadcasted_iota(jnp.int32, (count, rows), 0)
    expert = lax.shift_right_logical(place, slot_count.bit_length() - 1)
    slot = (place & (slot_count - 1)).astype(jnp.float32)
    label = lax.broadcasted_iota(jnp.int32, (experts, rows), 0)
    named = jnp.zeros((count, rows), jnp.float32)
    gate = jnp.zeros((count, rows), jnp.float32)
    chosen = jnp.zeros((experts, rows), jnp.float32)
    for j in range(top_count):
        route = routes_ref[j : j + 1, :]
        hit = expert == route
        named = named + jnp.where(hit, 1.0, 0.0)
        gate = gate + jnp.where(hit, gates_ref[j : j + 1, :], 0.0)
        chosen = chosen + jnp.where(label == route, 1.0, 0.0)
    row = lax.broadcasted_iota(jnp.int32, (rows, rows), 0)
    column = lax.broadcasted_iota(jnp.int32, (rows, rows), 1)
    earlier = jnp.where(row < column, 1.0, 0.0).astype(jnp.bfloat16)
    rank = jnp.dot(named.astype(jnp.bfloat16), earlier, preferred_element_type=jnp.float32)
    pick = jnp.where(rank == slot, gate, 0.0)
    high = pick.astype(jnp.bfloat16)
    low = (pick - high.astype(jnp.float32)).astype(jnp.bfloat16)
    pick_ref[...] = jnp.concatenate([high, low], axis=1)
    for sums_ref, values in ((counts_ref, chosen), (shares_ref, probs_ref[...])):
        sums = lax.dot_general(
            jnp.ones((8, rows), jnp.float32),
            values,
            (((1,), (1,)), ((), ())),
            precision=lax.Precision.HIGHEST,
            preferred_element_type=jnp.float32,
        )
        sums_ref[...] = sums[0:1]


def pick_matrix(routes, gates, probs, slot_count):
    experts, rows = probs.shape
    sums = jax.ShapeDtypeStruct((1, experts), jnp.float32)
    return pl.pallas_call(
        lambda *refs: pick_kernel(slot_count, *refs),
        out_shape=[
            jax.ShapeDtypeStruct((experts * slot_count, 2 * rows), jnp.bfloat16),
            sums,
            sums,
        ],
        compiler_params=pltpu.CompilerParams(vmem_limit_bytes=8 * MIB),
        name="pick_matrix",
    )(routes, gates, probs)


def combine_kernel(
    pick_ref,
    slots_ref,
    residual_ref,
    gain_ref,
    counts_ref,
    shares_ref,
    fresh_ref,
    normed_ref,
    ring_ref,
):
    rows, width = residual_ref.shape
    split = normed_ref.shape[1]
    block = 256
    total = jnp.zeros((rows, lanes), jnp.float32)
    pick = pick_ref[...]
    for start in range(0, width, block):
        at = pl.ds(start, block)
        both = lax.dot_general(
            pick,
            slots_ref[:, at],
            (((0,), (0,)), ((), ())),
            preferred_element_type=jnp.float32,
        )
        mixture = both[:rows] + both[rows:]
        fresh = (residual_ref[:, at].astype(jnp.float32) + mixture).astype(jnp.bfloat16)
        fresh_ref[:, at] = fresh
        values = fresh.astype(jnp.float32)
        square = values * values
        for lane in range(0, block, lanes):
            total = total + square[:, lane : lane + lanes]
    mean = jnp.sum(total, axis=1, keepdims=True) / width
    scale = lax.rsqrt(mean + eps)
    for start in range(0, width, block):
        at = pl.ds(start, block)
        values = fresh_ref[:, at].astype(jnp.float32)
        normed = (values * scale * gain_ref[:, at]).astype(jnp.bfloat16)
        if start < split:
            normed_ref[:, at] = normed
        else:
            ring_ref[:, pl.ds(start - split, block)] = normed
    row = lax.broadcasted_iota(jnp.int32, (rows, lanes), 0)
    riding = jnp.zeros((rows, lanes), jnp.float32)
    pad = jnp.zeros((1, lanes - counts_ref.shape[1]), jnp.float32)
    for base, ref in ((0, counts_ref), (3, shares_ref)):
        rest = jnp.concatenate([ref[...], pad], axis=1)
        for part in range(3):
            piece = rest.astype(jnp.bfloat16).astype(jnp.float32)
            rest = rest - piece
            riding = jnp.where(row == base + part, piece, riding)
    ring_ref[:, pl.ds(width - split, lanes)] = riding.astype(jnp.bfloat16)


def combine(pick, slots, residual, gain, counts, shares, split):
    rows, width = residual.shape
    return pl.pallas_call(
        combine_kernel,
        out_shape=[
            jax.ShapeDtypeStruct((rows, width), jnp.bfloat16),
            jax.ShapeDtypeStruct((rows, split), jnp.bfloat16),
            jax.ShapeDtypeStruct((rows, width - split + lanes), jnp.bfloat16),
        ],
        compiler_params=pltpu.CompilerParams(vmem_limit_bytes=16 * MIB),
        cost_estimate=pl.CostEstimate(
            flops=4 * rows * slots.shape[0] * width,
            bytes_accessed=2 * (slots.size + 3 * residual.size),
            transcendentals=0,
        ),
        name="combine_and_norm",
    )(pick, slots, residual, gain, counts, shares)


def ring_kernel(
    rows, factors, me_ref, weight_ref, own_ref, other_ref, sums_ref, balance_ref, held_ref
):
    chips = own_ref.shape[0] // rows
    share = own_ref.shape[1] - lanes
    chip = lax.shift_right_logical(me_ref[0], 1)
    first = (me_ref[0] & 1) == 0
    for step in range(chips):
        own = own_ref[step * rows : (step + 1) * rows, :]
        other = other_ref[step * rows : (step + 1) * rows, :]
        source = lax.rem(chip - step + chips, chips)
        pair = jnp.concatenate([jnp.where(first, own, other), jnp.where(first, other, own)], axis=0)
        held_ref[pl.ds(pl.multiple_of(source * 2 * rows, 2 * rows), 2 * rows), :] = pair
    sums_ref[...] = lax.dot_general(
        weight_ref[:, pl.ds(weight_ref.shape[1] - share, share)],
        held_ref[:, pl.ds(0, share)],
        (((1,), (1,)), ((), ())),
        preferred_element_type=jnp.float32,
    )
    riding = jnp.zeros((16, lanes), jnp.float32)
    for source in range(2 * chips):
        riding = riding + held_ref[pl.ds(source * rows, 16), pl.ds(share, lanes)].astype(jnp.float32)
    tokens_of, pairs_of, experts = factors
    usage = (riding[0:1] + riding[1:2] + riding[2:3]) / pairs_of
    shares = (riding[3:4] + riding[4:5] + riding[5:6]) / tokens_of
    balance_ref[...] = experts * jnp.sum(usage * shares, axis=1, keepdims=True)


def ring_project(me, weight_t, own, other, rows, factors):
    columns, width = weight_t.shape
    count, share = 2 * own.shape[0], own.shape[1] - lanes
    vmem = pl.BlockSpec(memory_space=pltpu.VMEM)
    return pl.pallas_call(
        lambda *refs: ring_kernel(rows, factors, *refs),
        in_specs=[pl.BlockSpec(memory_space=pltpu.SMEM), vmem, vmem, vmem],
        out_specs=[vmem, vmem],
        out_shape=[
            jax.ShapeDtypeStruct((columns, count), jnp.float32),
            jax.ShapeDtypeStruct((1, 1), jnp.float32),
        ],
        scratch_shapes=[pltpu.VMEM((count, own.shape[1]), jnp.bfloat16)],
        compiler_params=pltpu.CompilerParams(vmem_limit_bytes=24 * MIB),
        cost_estimate=pl.CostEstimate(
            flops=2 * count * share * columns,
            bytes_accessed=2 * (count * share + columns * (width + 2 * count)),
            transcendentals=0,
        ),
        name="ring_project",
    )(me, weight_t, own, other)


def project_kernel(weight_ref, rows_ref, sums_ref, out_ref):
    product = lax.dot_general(
        weight_ref[...],
        rows_ref[...],
        (((1,), (1,)), ((), ())),
        preferred_element_type=jnp.float32,
    )
    out_ref[...] = (product + sums_ref[...]).astype(jnp.bfloat16)


def project(weight_t, gathered, sums, steps=2):
    count, share = gathered.shape
    columns = weight_t.shape[0]
    block = count // steps
    return pl.pallas_call(
        project_kernel,
        grid=(steps,),
        in_specs=[
            pl.BlockSpec((columns, share), lambda i: (0, 0)),
            pl.BlockSpec((block, share), lambda i: (i, 0)),
            pl.BlockSpec((columns, block), lambda i: (0, i)),
        ],
        out_specs=pl.BlockSpec((columns, block), lambda i: (0, i)),
        out_shape=jax.ShapeDtypeStruct((columns, count), jnp.bfloat16),
        compiler_params=pltpu.CompilerParams(vmem_limit_bytes=56 * MIB),
        cost_estimate=pl.CostEstimate(
            flops=2 * count * share * columns,
            bytes_accessed=2 * (count * share + columns * (share + 3 * count)),
            transcendentals=0,
        ),
        name="qkv_project",
    )(weight_t, gathered, sums)


def on_device(
    residual, expert_hidden, down_weight, gates, routes, router_probs, norm_gain, qkv_weight
):
    experts = lax.axis_size("tensor")
    rows, width = residual.shape
    slot_count = expert_hidden.shape[1] // experts
    split = width * 3 // 4
    expert_out = expert_project(expert_hidden[0], down_weight[0])
    returned = lax.all_to_all(
        expert_out.reshape(experts, slot_count, width),
        "tensor",
        split_axis=0,
        concat_axis=0,
        tiled=True,
    ).reshape(experts * slot_count, width)
    pick, counts, shares = pick_matrix(routes.T, gates.T, router_probs.T, slot_count)
    depth = 16
    breadth = lax.axis_size("dp") // depth
    lines = [[x * depth + z for z in range(depth)] for x in range(breadth)]
    cross = [[x * depth + z for x in range(breadth)] for z in range(depth)]
    sums = lax.psum((counts, shares), "dp", axis_index_groups=cross)
    sums = lax.psum(sums, "dp", axis_index_groups=lines)
    fresh, normed, riding = combine(
        pick, returned, residual, norm_gain.reshape(1, width), *sums, split
    )
    gathered = lax.all_gather(normed, "tensor", axis=0, tiled=True)
    chips = experts // 2
    up = [(i, (i + 2) % experts) for i in range(experts)]
    down = [(i, (i - 2) % experts) for i in range(experts)]
    ups, downs = [riding], [riding]
    for step in range(chips // 2):
        ups.append(lax.ppermute(ups[-1], "tensor", up))
        if step < chips // 2 - 1:
            downs.append(lax.ppermute(downs[-1], "tensor", down))
    own = jnp.concatenate(ups + downs[:0:-1], axis=0)
    other = lax.ppermute(own, "tensor", [(i, i ^ 1) for i in range(experts)])
    total_tokens = rows * lax.axis_size("dp") * experts
    factors = (float(total_tokens), float(total_tokens * routes.shape[1]), float(experts))
    me = lax.axis_index("tensor").astype(jnp.int32).reshape(1)
    weight_t = qkv_weight.T
    part, balance = ring_project(me, weight_t, own, other, rows, factors)
    projected = project(weight_t, gathered, part).T
    return (fresh, projected, balance.reshape(()))


def solution(mesh):
    in_specs = (
        P(("dp", "tensor"), None),
        P(("dp", "tensor"), None, None),
        P("tensor", None, None),
        P(("dp", "tensor"), None),
        P(("dp", "tensor"), None),
        P(("dp", "tensor"), None),
        P(),
        P(None, "tensor"),
    )
    out_specs = (P(("dp", "tensor"), None), P("dp", "tensor"), P())
    return jax.shard_map(
        on_device, mesh=mesh, in_specs=in_specs, out_specs=out_specs, check_vma=False
    )
```

time: 162 us -> 150 us (0.926)
  starting transfers between devices: 17.8 us -> 45.8 us
  blocking collectives: 61.9 us -> 38.5 us
  waiting for transfers between devices: 43.6 us -> 28.9 us
    all_gather x1, waiting for transfers between devices: 35.5 us -> 3.11 us  [on_device(): gathered = lax.all_gather(normed, 'tensor', axis=0, tiled=True)]
    ppermute x0 -> x8, starting transfers between devices: none -> 28 us  [the longest x3 14.6 us: on_device(): downs.append(lax.ppermute(downs[-1], 'tensor', down))]
    psum x1 -> x0, blocking collectives: 23.4 us -> none  [on_device(): totals = lax.psum((counts, shares), 'tensor')]
    ppermute x0 -> x8, waiting for transfers between devices: none -> 15.6 us  [the longest x4 10.9 us: on_device(): ups.append(lax.ppermute(ups[-1], 'tensor', up))]
    all_to_all x1, waiting for transfers between devices: 8.1 us -> 10.2 us  [on_device(): lax.all_to_all(expert_out.reshape(experts, slot_count, width), 'tensor',...]
    pallas_call x3 -> x4, Pallas kernels: 15.1 us -> 14.3 us  [the longest x1 5.88 us: project(): pl.pallas_call(project_kernel, grid=(steps,), in_specs=[pl.BlockSpec((col...]
    unnamed x17 -> x21, local copies, waits for them, and re-layouts: 5.03 us -> 5.79 us
  transfers between devices with their start and end apart: 2 -> 10, of which waited for: 2 -> 7; matrix products, arithmetic and copies ran while one was open for 1% -> 4% of each run, Pallas kernels for 1% -> 2%
where the time goes in v2:
time: 150 us
  starting transfers between devices  45.8 us (31%)
  blocking collectives  38.5 us (26%)
  waiting for transfers between devices  28.9 us (19%)
  Pallas kernels  15.7 us (10%)
  between operations  14.2 us (9%)
  local copies, waits for them, and re-layouts  6.46 us (4%)
    psum x1, blocking collectives, on_device(): sums = lax.psum(sums, 'dp', axis_index_groups=lines)  31.9 us
    all_to_all x1, starting transfers between devices, on_device(): lax.all_to_all(expert_out.reshape(experts, slot_count, width), 'tensor',...  17.8 us
    ppermute x3, starting transfers between devices, on_device(): downs.append(lax.ppermute(downs[-1], 'tensor', down))  14.6 us
    ppermute x4, waiting for transfers between devices, on_device(): ups.append(lax.ppermute(ups[-1], 'tensor', up))  10.9 us
    all_to_all x1, waiting for transfers between devices, on_device(): lax.all_to_all(expert_out.reshape(experts, slot_count, width), 'tensor',...  10.2 us
    ppermute x4, starting transfers between devices, on_device(): ups.append(lax.ppermute(ups[-1], 'tensor', up))  7.78 us
    psum x1, blocking collectives, on_device(): sums = lax.psum((counts, shares), 'dp', axis_index_groups=cross)  6.6 us
    pallas_call x1, Pallas kernels, project(): pl.pallas_call(project_kernel, grid=(steps,), in_specs=[pl.BlockSpec((col...  5.88 us
  transfers between devices with their start and end apart: 10, of which 7 were waited for; matrix products, arithmetic and copies ran while one was open for 4% of the time, Pallas kernels for 2%

profile of v2, /device:TPU:1, one launch (start us, length us, event | category | flops | bytes accessed | tf_op | source)
XLA Modules:
  0.0 149.6 jit_solution(16180766203945766440)
XLA Ops:
  7.2 5.0 %expert_project.1 = bf16[256,4096]{1,0:T(8,128)(2,1)} custom-call(bf16[256,768]{1,0:T(8,128)(2,1)} %bitcast.22, bf16[768,4096]{1,0:T(8,128)(2,1)} %bitcast.20), custom_call_target="tpu_custom_call" | custom-call | flops 1610612736 | bytes 8781824 | tf_op jit(solution)/shard_map/expert_project/pallas_call | solution.py:32
  12.2 17.8 %all-to-all-start = ((bf16[16,16,4096]{2,1,0:T(8,128)(2,1)}), bf16[16,16,4096]{2,1,0:T(8,128)(2,1)S(1)}, u32[]{:S(2)}, u32[]{:S(2)}) async-start(bf16[16,16,4096]{2,1,0:T(8,128)(2,1)} %bitcast.19), calls=%async_computation | async-start | bytes 4194304 | tf_op jit(solution)/shard_map/all_to_all | solution.py:265
  30.0 0.2 pick_matrix.1
  30.3 6.6 %all-reduce.1 = (f32[1,16]{1,0:T(1,128)S(1)}, f32[1,16]{1,0:T(1,128)S(1)}) all-reduce(f32[1,16]{1,0:T(1,128)S(1)} %get-tuple-element.12, f32[1,16]{1,0:T(1,128)S(1)} %get-tuple-element.13), channel_id=1, replica_groups={{0,256,512,768},{16,272,528,784},{32,288,544,800},{48,304,560,816},{64,..., use_global_device_ids=true, to_apply=%region_0.0 | all-reduce | flops 32 | bytes 256 | tf_op jit(solution)/shard_map/psum | solution.py:277
  36.9 31.9 %all-reduce = (f32[1,16]{1,0:T(1,128)S(1)}, f32[1,16]{1,0:T(1,128)S(1)}) all-reduce(f32[1,16]{1,0:T(1,128)S(1)} %get-tuple-element.21, f32[1,16]{1,0:T(1,128)S(1)} %get-tuple-element.22), channel_id=1, replica_groups={{0,16,32,48,64,80,96,112,128,144,160,176,192,208,224,240},{256,272,288,..., use_global_device_ids=true, to_apply=%region_1.0 | all-reduce | flops 32 | bytes 256 | tf_op jit(solution)/shard_map/psum | solution.py:278
  68.8 10.2 %all-to-all-done = bf16[16,16,4096]{2,1,0:T(8,128)(2,1)S(1)} async-done(((bf16[16,16,4096]{2,1,0:T(8,128)(2,1)}), bf16[16,16,4096]{2,1,0:T(8,128)(2,1)S(1)}, u32[]{:S(2)}, u32[]{:S(2)}) %all-to-all-start) | async-done | bytes 2097184 | tf_op jit(solution)/shard_map/all_to_all | solution.py:265
  79.0 1.4 combine_and_norm.1
  80.4 2.1 %collective-permute-start = (bf16[64,1152]{1,0:T(8,128)(2,1)S(1)}, bf16[64,1152]{1,0:T(8,128)(2,1)S(1)}, u32[]{:S(2)}, u32[]{:S(2)}) collective-permute-start(bf16[64,1152]{1,0:T(8,128)(2,1)S(1)} %get-tuple-element.16), channel_id=1, source_target_pairs={{0,2},{1,3},{2,4},{3,5},{4,6},{5,7},{6,8},{7,9},{8,10},{9,11},{10,... | collective-permute-start | bytes 442376 | tf_op jit(solution)/shard_map/ppermute | solution.py:288
  82.5 4.6 %collective-permute-start.4 = (bf16[64,1152]{1,0:T(8,128)(2,1)S(1)}, bf16[64,1152]{1,0:T(8,128)(2,1)S(1)}, u32[]{:S(2)}, u32[]{:S(2)}) collective-permute-start(bf16[64,1152]{1,0:T(8,128)(2,1)S(1)} %get-tuple-element.16), channel_id=1, source_target_pairs={{0,14},{1,15},{2,0},{3,1},{4,2},{5,3},{6,4},{7,5},{8,6},{9,7},{10,... | collective-permute-start | bytes 442376 | tf_op jit(solution)/shard_map/ppermute | solution.py:290
  87.0 0.7 constant_dynamic-update-slice_fusion.7
  87.7 1.0 collective-permute-done
  88.7 1.9 %collective-permute-start.1 = (bf16[64,1152]{1,0:T(8,128)(2,1)S(1)}, bf16[64,1152]{1,0:T(8,128)(2,1)S(1)}, u32[]{:S(2)}, u32[]{:S(2)}) collective-permute-start(bf16[64,1152]{1,0:T(8,128)(2,1)S(1)} %collective-permute-done), channel_id=1, source_target_pairs={{0,2},{1,3},{2,4},{3,5},{4,6},{5,7},{6,8},{7,9},{8,10},{9,11},{10,... | collective-permute-start | bytes 442376 | tf_op jit(solution)/shard_map/ppermute | solution.py:288
  90.6 4.6 %collective-permute-start.5 = (bf16[64,1152]{1,0:T(8,128)(2,1)S(1)}, bf16[64,1152]{1,0:T(8,128)(2,1)S(1)}, u32[]{:S(2)}, u32[]{:S(2)}) collective-permute-start(bf16[64,1152]{1,0:T(8,128)(2,1)S(1)} %collective-permute-done.4), channel_id=1, source_target_pairs={{0,14},{1,15},{2,0},{3,1},{4,2},{5,3},{6,4},{7,5},{8,6},{9,7},{10,... | collective-permute-start | bytes 442376 | tf_op jit(solution)/shard_map/ppermute | solution.py:290
  95.2 0.7 constant_dynamic-update-slice_fusion.6
  95.9 1.9 %collective-permute-start.2 = (bf16[64,1152]{1,0:T(8,128)(2,1)S(1)}, bf16[64,1152]{1,0:T(8,128)(2,1)S(1)}, u32[]{:S(2)}, u32[]{:S(2)}) collective-permute-start(bf16[64,1152]{1,0:T(8,128)(2,1)S(1)} %collective-permute-done.1), channel_id=1, source_target_pairs={{0,2},{1,3},{2,4},{3,5},{4,6},{5,7},{6,8},{7,9},{8,10},{9,11},{10,... | collective-permute-start | bytes 442376 | tf_op jit(solution)/shard_map/ppermute | solution.py:288
  97.8 1.8 %collective-permute-done.5 = bf16[64,1152]{1,0:T(8,128)(2,1)S(1)} collective-permute-done((bf16[64,1152]{1,0:T(8,128)(2,1)S(1)}, bf16[64,1152]{1,0:T(8,128)(2,1)S(1)}, u32[]{:S(2)}, u32[]{:S(2)}) %collective-permute-start.5) | collective-permute-done | bytes 147488 | tf_op jit(solution)/shard_map/ppermute | solution.py:290
  99.5 5.4 %collective-permute-start.6 = (bf16[64,1152]{1,0:T(8,128)(2,1)S(1)}, bf16[64,1152]{1,0:T(8,128)(2,1)S(1)}, u32[]{:S(2)}, u32[]{:S(2)}) collective-permute-start(bf16[64,1152]{1,0:T(8,128)(2,1)S(1)} %collective-permute-done.5), channel_id=1, source_target_pairs={{0,14},{1,15},{2,0},{3,1},{4,2},{5,3},{6,4},{7,5},{8,6},{9,7},{10,... | collective-permute-start | bytes 442376 | tf_op jit(solution)/shard_map/ppermute | solution.py:290
  105.0 0.7 constant_dynamic-update-slice_fusion.5
  105.6 1.5 %collective-permute-done.2 = bf16[64,1152]{1,0:T(8,128)(2,1)S(1)} collective-permute-done((bf16[64,1152]{1,0:T(8,128)(2,1)S(1)}, bf16[64,1152]{1,0:T(8,128)(2,1)S(1)}, u32[]{:S(2)}, u32[]{:S(2)}) %collective-permute-start.2) | collective-permute-done | bytes 147488 | tf_op jit(solution)/shard_map/ppermute | solution.py:288
  107.1 1.9 %collective-permute-start.3 = (bf16[64,1152]{1,0:T(8,128)(2,1)S(1)}, bf16[64,1152]{1,0:T(8,128)(2,1)S(1)}, u32[]{:S(2)}, u32[]{:S(2)}) collective-permute-start(bf16[64,1152]{1,0:T(8,128)(2,1)S(1)} %collective-permute-done.2), channel_id=1, source_target_pairs={{0,2},{1,3},{2,4},{3,5},{4,6},{5,7},{6,8},{7,9},{8,10},{9,11},{10,... | collective-permute-start | bytes 442376 | tf_op jit(solution)/shard_map/ppermute | solution.py:288
  109.1 0.7 constant_dynamic-update-slice_fusion.4
  109.7 8.4 %collective-permute-done.3 = bf16[64,1152]{1,0:T(8,128)(2,1)S(1)} collective-permute-done((bf16[64,1152]{1,0:T(8,128)(2,1)S(1)}, bf16[64,1152]{1,0:T(8,128)(2,1)S(1)}, u32[]{:S(2)}, u32[]{:S(2)}) %collective-permute-start.3) | collective-permute-done | bytes 147488 | tf_op jit(solution)/shard_map/ppermute | solution.py:288
  118.2 0.7 constant_dynamic-update-slice_fusion.3
  118.9 0.7 constant_dynamic-update-slice_fusion.2
  119.5 0.7 constant_dynamic-update-slice_fusion.1
  120.2 0.7 constant_dynamic-update-slice_fusion.refs_2_
  120.9 5.7 %collective-permute-start.7 = (bf16[512,1152]{1,0:T(8,128)(2,1)}, bf16[512,1152]{1,0:T(8,128)(2,1)}, u32[]{:S(2)}, u32[]{:S(2)}) collective-permute-start(bf16[512,1152]{1,0:T(8,128)(2,1)} %constant_dynamic-update-slice_fusion.refs_2_), channel_id=1, source_target_pairs={{0,1},{1,0},{2,3},{3,2},{4,5},{5,4},{6,7},{7,6},{8,9},{9,8},{10,11... | collective-permute-start | bytes 3538952 | tf_op jit(solution)/shard_map/ppermute | solution.py:292
  126.6 2.9 %collective-permute-done.7.refs_3_ = bf16[512,1152]{1,0:T(8,128)(2,1)} collective-permute-done((bf16[512,1152]{1,0:T(8,128)(2,1)}, bf16[512,1152]{1,0:T(8,128)(2,1)}, u32[]{:S(2)}, u32[]{:S(2)}) %collective-permute-start.7) | collective-permute-done | bytes 1179680 | tf_op jit(solution)/shard_map/ppermute | solution.py:292
  129.5 3.2 %ring_project.1 = (f32[320,1024]{1,0:T(8,128)S(1)}, f32[1,1]{1,0:T(1,128)}) custom-call(s32[1]{0:T(128)} %bitcast.9.refs_0_, bf16[320,4096]{1,0:T(8,128)(2,1)S(1)} %bitcast.13, bf16[512,1152]{1,0:T(8,128)(2,1)} %constant_dynamic-update-slice_fusion.refs_2_, bf16[512,1152]{1,0:T(8,128)(2,1)} %collective-permute-done.7.refs_3_), custom_call_target="tpu_custom_call" | custom-call | flops 671088640 | bytes 6029312 | tf_op jit(solution)/shard_map/ring_project/pallas_call | solution.py:204
  132.7 1.1 copy-done.1
  133.8 3.1 %all-gather.2.cloned.1.call-done.rows_ref = bf16[1024,3072]{1,0:T(8,128)(2,1)} async-done(((bf16[64,3072]{1,0:T(8,128)(2,1)}), bf16[1024,3072]{1,0:T(8,128)(2,1)}) %all-gather.2.cloned.1.call-update) | async-done | bytes 6291472 | tf_op jit(solution)/shard_map/all_gather | solution.py:282
  136.9 5.9 %qkv_project.1 = bf16[320,1024]{1,0:T(8,128)(2,1)} custom-call(bf16[320,4096]{1,0:T(8,128)(2,1)} %bitcast.12, bf16[1024,3072]{1,0:T(8,128)(2,1)} %all-gather.2.cloned.1.call-done.rows_ref, f32[320,1024]{1,0:T(8,128)} %copy-done.1), custom_call_target="tpu_custom_call" | custom-call | flops 2013265920 | bytes 10223616 | tf_op jit(solution)/shard_map/qkv_project/pallas_call | solution.py:237
  (18 shorter events, 0.1 us)
Async XLA Ops:
  12.1 17.9 %copy-start.4 = (f32[64,16]{0,1:T(8,128)S(1)}, f32[64,16]{0,1:T(8,128)}, u32[]{:S(2)}) copy-start(f32[64,16]{0,1:T(8,128)} %param.13) | copy-start | bytes 12292
  12.1 17.9 %copy-start.5 = (s32[64,2]{0,1:T(2,128)S(1)}, s32[64,2]{0,1:T(2,128)}, u32[]{:S(2)}) copy-start(s32[64,2]{0,1:T(2,128)} %param.12) | copy-start | bytes 1540
  12.1 17.9 %copy-start.6 = (f32[64,2]{0,1:T(2,128)S(1)}, f32[64,2]{0,1:T(2,128)}, u32[]{:S(2)}) copy-start(f32[64,2]{0,1:T(2,128)} %param.11) | copy-start | bytes 1540
  12.1 66.8 %copy-start.2 = (bf16[64,4096]{1,0:T(8,128)(2,1)S(1)}, bf16[64,4096]{1,0:T(8,128)(2,1)}, u32[]{:S(2)}) copy-start(bf16[64,4096]{1,0:T(8,128)(2,1)} %residual_ref.1) | copy-start | bytes 1572868
  12.1 66.8 %copy-start.3 = (f32[4096]{0:T(1024)S(1)}, f32[4096]{0:T(1024)}, u32[]{:S(2)}) copy-start(f32[4096]{0:T(1024)} %param.14) | copy-start | bytes 49156
  12.2 66.8 %all-to-all-start = ((bf16[16,16,4096]{2,1,0:T(8,128)(2,1)}), bf16[16,16,4096]{2,1,0:T(8,128)(2,1)S(1)}, u32[]{:S(2)}, u32[]{:S(2)}) async-start(bf16[16,16,4096]{2,1,0:T(8,128)(2,1)} %bitcast.19), calls=%async_computation | async-start | bytes 4194304 | tf_op jit(solution)/shard_map/all_to_all | solution.py:265
  30.0 106.9 %all-gather.2.cloned.1.call-start = ((), (), s32[]{:S(2)}) async-start(), calls=%async_computation.1 | async-start | bytes 6684672 | tf_op jit(solution)/shard_map/all_gather | solution.py:282
  80.4 49.1 %copy-start = (bf16[4096,320]{0,1:T(8,128)(2,1)S(1)}, bf16[4096,320]{0,1:T(8,128)(2,1)}, u32[]{:S(2)}) copy-start(bf16[4096,320]{0,1:T(8,128)(2,1)} %param.15) | copy-start | bytes 7864324
  80.4 8.3 %collective-permute-start = (bf16[64,1152]{1,0:T(8,128)(2,1)S(1)}, bf16[64,1152]{1,0:T(8,128)(2,1)S(1)}, u32[]{:S(2)}, u32[]{:S(2)}) collective-permute-start(bf16[64,1152]{1,0:T(8,128)(2,1)S(1)} %get-tuple-element.16), channel_id=1, source_target_pairs={{0,2},{1,3},{2,4},{3,5},{4,6},{5,7},{6,8},{7,9},{8,10},{9,11},{10,... | collective-permute-start | bytes 442376 | tf_op jit(solution)/shard_map/ppermute | solution.py:288
  82.5 8.1 %collective-permute-start.4 = (bf16[64,1152]{1,0:T(8,128)(2,1)S(1)}, bf16[64,1152]{1,0:T(8,128)(2,1)S(1)}, u32[]{:S(2)}, u32[]{:S(2)}) collective-permute-start(bf16[64,1152]{1,0:T(8,128)(2,1)S(1)} %get-tuple-element.16), channel_id=1, source_target_pairs={{0,14},{1,15},{2,0},{3,1},{4,2},{5,3},{6,4},{7,5},{8,6},{9,7},{10,... | collective-permute-start | bytes 442376 | tf_op jit(solution)/shard_map/ppermute | solution.py:290
  88.7 7.2 %collective-permute-start.1 = (bf16[64,1152]{1,0:T(8,128)(2,1)S(1)}, bf16[64,1152]{1,0:T(8,128)(2,1)S(1)}, u32[]{:S(2)}, u32[]{:S(2)}) collective-permute-start(bf16[64,1152]{1,0:T(8,128)(2,1)S(1)} %collective-permute-done), channel_id=1, source_target_pairs={{0,2},{1,3},{2,4},{3,5},{4,6},{5,7},{6,8},{7,9},{8,10},{9,11},{10,... | collective-permute-start | bytes 442376 | tf_op jit(solution)/shard_map/ppermute | solution.py:288
  90.6 8.9 %collective-permute-start.5 = (bf16[64,1152]{1,0:T(8,128)(2,1)S(1)}, bf16[64,1152]{1,0:T(8,128)(2,1)S(1)}, u32[]{:S(2)}, u32[]{:S(2)}) collective-permute-start(bf16[64,1152]{1,0:T(8,128)(2,1)S(1)} %collective-permute-done.4), channel_id=1, source_target_pairs={{0,14},{1,15},{2,0},{3,1},{4,2},{5,3},{6,4},{7,5},{8,6},{9,7},{10,... | collective-permute-start | bytes 442376 | tf_op jit(solution)/shard_map/ppermute | solution.py:290
  95.9 11.3 %collective-permute-start.2 = (bf16[64,1152]{1,0:T(8,128)(2,1)S(1)}, bf16[64,1152]{1,0:T(8,128)(2,1)S(1)}, u32[]{:S(2)}, u32[]{:S(2)}) collective-permute-start(bf16[64,1152]{1,0:T(8,128)(2,1)S(1)} %collective-permute-done.1), channel_id=1, source_target_pairs={{0,2},{1,3},{2,4},{3,5},{4,6},{5,7},{6,8},{7,9},{8,10},{9,11},{10,... | collective-permute-start | bytes 442376 | tf_op jit(solution)/shard_map/ppermute | solution.py:288
  99.5 19.3 %collective-permute-start.6 = (bf16[64,1152]{1,0:T(8,128)(2,1)S(1)}, bf16[64,1152]{1,0:T(8,128)(2,1)S(1)}, u32[]{:S(2)}, u32[]{:S(2)}) collective-permute-start(bf16[64,1152]{1,0:T(8,128)(2,1)S(1)} %collective-permute-done.5), channel_id=1, source_target_pairs={{0,14},{1,15},{2,0},{3,1},{4,2},{5,3},{6,4},{7,5},{8,6},{9,7},{10,... | collective-permute-start | bytes 442376 | tf_op jit(solution)/shard_map/ppermute | solution.py:290
  107.1 11.0 %collective-permute-start.3 = (bf16[64,1152]{1,0:T(8,128)(2,1)S(1)}, bf16[64,1152]{1,0:T(8,128)(2,1)S(1)}, u32[]{:S(2)}, u32[]{:S(2)}) collective-permute-start(bf16[64,1152]{1,0:T(8,128)(2,1)S(1)} %collective-permute-done.2), channel_id=1, source_target_pairs={{0,2},{1,3},{2,4},{3,5},{4,6},{5,7},{6,8},{7,9},{8,10},{9,11},{10,... | collective-permute-start | bytes 442376 | tf_op jit(solution)/shard_map/ppermute | solution.py:288
  120.9 8.6 %collective-permute-start.7 = (bf16[512,1152]{1,0:T(8,128)(2,1)}, bf16[512,1152]{1,0:T(8,128)(2,1)}, u32[]{:S(2)}, u32[]{:S(2)}) collective-permute-start(bf16[512,1152]{1,0:T(8,128)(2,1)} %constant_dynamic-update-slice_fusion.refs_2_), channel_id=1, source_target_pairs={{0,1},{1,0},{2,3},{3,2},{4,5},{5,4},{6,7},{7,6},{8,9},{9,8},{10,11... | collective-permute-start | bytes 3538952 | tf_op jit(solution)/shard_map/ppermute | solution.py:292
  132.7 1.1 copy-start.1
Sparse Core Ops, SparseCore 0:
  80.5 56.2 all-gather.1

commit v3 on v2

v3 whole, which is shorter than its diff:
```python
import jax
import jax.numpy as jnp
from jax import lax
from jax.experimental import pallas as pl
from jax.experimental.pallas import tpu as pltpu
from jax.sharding import PartitionSpec as P

eps = 1e-06
lanes = 128
scale_lane = 64
MIB = 2**20


def expert_kernel(hidden_ref, weight_ref, out_ref):
    out_ref[...] = jnp.dot(
        hidden_ref[...], weight_ref[...], preferred_element_type=jnp.float32
    ).astype(jnp.bfloat16)


def expert_project(hidden, weight, start, width, steps):
    slots, depth = hidden.shape
    block = width // steps
    return pl.pallas_call(
        expert_kernel,
        grid=(steps,),
        in_specs=[
            pl.BlockSpec((slots, depth), lambda i: (0, 0)),
            pl.BlockSpec((depth, block), lambda i: (0, start // block + i)),
        ],
        out_specs=pl.BlockSpec((slots, block), lambda i: (0, i)),
        out_shape=jax.ShapeDtypeStruct((slots, width), jnp.bfloat16),
        compiler_params=pltpu.CompilerParams(vmem_limit_bytes=56 * MIB),
        cost_estimate=pl.CostEstimate(
            flops=2 * slots * depth * width,
            bytes_accessed=2 * (depth * width + slots * (depth + width)),
            transcendentals=0,
        ),
        name="expert_project",
    )(hidden, weight)


def pick_kernel(
    slot_count, routes_ref, gates_ref, probs_ref, _, pick_ref, sums_ref
):
    top_count, rows = routes_ref.shape
    experts = probs_ref.shape[0]
    count = experts * slot_count
    place = lax.broadcasted_iota(jnp.int32, (count, rows), 0)
    expert = lax.shift_right_logical(place, slot_count.bit_length() - 1)
    slot = (place & (slot_count - 1)).astype(jnp.float32)
    label = lax.broadcasted_iota(jnp.int32, (experts, rows), 0)
    named = jnp.zeros((count, rows), jnp.float32)
    gate = jnp.zeros((count, rows), jnp.float32)
    chosen = jnp.zeros((experts, rows), jnp.float32)
    for j in range(top_count):
        route = routes_ref[j : j + 1, :]
        hit = expert == route
        named = named + jnp.where(hit, 1.0, 0.0)
        gate = gate + jnp.where(hit, gates_ref[j : j + 1, :], 0.0)
        chosen = chosen + jnp.where(label == route, 1.0, 0.0)
    row = lax.broadcasted_iota(jnp.int32, (rows, rows), 0)
    column = lax.broadcasted_iota(jnp.int32, (rows, rows), 1)
    earlier = jnp.where(row < column, 1.0, 0.0).astype(jnp.bfloat16)
    rank = jnp.dot(named.astype(jnp.bfloat16), earlier, preferred_element_type=jnp.float32)
    pick = jnp.where(rank == slot, gate, 0.0)
    high = pick.astype(jnp.bfloat16)
    low = (pick - high.astype(jnp.float32)).astype(jnp.bfloat16)
    pick_ref[...] = jnp.concatenate([high, low], axis=1)
    for place, values in enumerate((chosen, probs_ref[...])):
        sums = lax.dot_general(
            jnp.ones((8, rows), jnp.float32),
            values,
            (((1,), (1,)), ((), ())),
            precision=lax.Precision.HIGHEST,
            preferred_element_type=jnp.float32,
        )
        sums_ref[place : place + 1, :] = sums[0:1]


def pick_matrix(routes, gates, probs, before, slot_count):
    experts, rows = probs.shape
    return pl.pallas_call(
        lambda *refs: pick_kernel(slot_count, *refs),
        in_specs=[pl.BlockSpec(memory_space=pltpu.VMEM)] * 3
        + [pl.BlockSpec(memory_space=pl.ANY)],
        out_shape=[
            jax.ShapeDtypeStruct((experts * slot_count, 2 * rows), jnp.bfloat16),
            jax.ShapeDtypeStruct((2, experts), jnp.float32),
        ],
        compiler_params=pltpu.CompilerParams(vmem_limit_bytes=8 * MIB),
        name="pick_matrix",
    )(routes, gates, probs, before)


def combine_block(pick_ref, slots_ref, residual_ref, gain_ref, start, at, block):
    rows = residual_ref.shape[0]
    both = lax.dot_general(
        pick_ref[...],
        slots_ref[:, pl.ds(at, block)],
        (((0,), (0,)), ((), ())),
        preferred_element_type=jnp.float32,
    )
    mixture = both[:rows] + both[rows:]
    columns = pl.ds(start + at, block)
    fresh = (residual_ref[:, columns].astype(jnp.float32) + mixture).astype(jnp.bfloat16)
    values = fresh.astype(jnp.float32)
    scaled = (values * gain_ref[:, columns]).astype(jnp.bfloat16)
    return fresh, scaled


def first_kernel(
    pick_ref, slots_ref, residual_ref, gain_ref, sums_ref, head_ref, scaled_ref, sums_out_ref
):
    sums_out_ref[...] = sums_ref[...]
    block = 256
    split, width = scaled_ref.shape[1], residual_ref.shape[1]
    for at in range(0, split, block):
        fresh, scaled = combine_block(pick_ref, slots_ref, residual_ref, gain_ref, 0, at, block)
        head_ref[:, pl.ds(at, block)] = fresh
        scaled_ref[:, pl.ds(at, block)] = scaled
    head_ref[:, pl.ds(split, width - split)] = residual_ref[:, pl.ds(split, width - split)]


def combine_first(pick, slots, residual, gain, sums):
    rows, width = residual.shape
    split = slots.shape[1]
    return pl.pallas_call(
        first_kernel,
        out_shape=[
            jax.ShapeDtypeStruct((rows, width), jnp.bfloat16),
            jax.ShapeDtypeStruct((rows, split), jnp.bfloat16),
            jax.ShapeDtypeStruct(sums.shape, jnp.float32),
        ],
        compiler_params=pltpu.CompilerParams(vmem_limit_bytes=16 * MIB),
        cost_estimate=pl.CostEstimate(
            flops=4 * rows * slots.shape[0] * split,
            bytes_accessed=2 * (slots.size + 3 * rows * width),
            transcendentals=0,
        ),
        name="combine_first",
    )(pick, slots, residual, gain, sums)


def last_kernel(pick_ref, slots_ref, head_ref, gain_ref, sums_ref, fresh_ref, ring_ref):
    rows, width = head_ref.shape
    share = slots_ref.shape[1]
    split = width - share
    block = 256
    total = jnp.zeros((rows, lanes), jnp.float32)
    for start in range(0, width, block):
        columns = pl.ds(start, block)
        if start < split:
            fresh = head_ref[:, columns]
        else:
            at = start - split
            fresh, scaled = combine_block(
                pick_ref, slots_ref, head_ref, gain_ref, split, at, block
            )
            ring_ref[:, pl.ds(at, block)] = scaled
        fresh_ref[:, columns] = fresh
        values = fresh.astype(jnp.float32)
        square = values * values
        for lane in range(0, block, lanes):
            total = total + square[:, lane : lane + lanes]
    mean = jnp.sum(total, axis=1, keepdims=True) / width
    scale = lax.rsqrt(mean + eps)
    row = lax.broadcasted_iota(jnp.int32, (rows, lanes), 0)
    lane = lax.broadcasted_iota(jnp.int32, (rows, lanes), 1)
    riding = jnp.zeros((rows, lanes), jnp.float32)
    pad = jnp.zeros((1, lanes - sums_ref.shape[1]), jnp.float32)
    for place in range(2):
        rest = jnp.concatenate([sums_ref[place : place + 1, :], pad], axis=1)
        for part in range(3):
            piece = rest.astype(jnp.bfloat16).astype(jnp.float32)
            rest = rest - piece
            riding = jnp.where(row == 3 * place + part, piece, riding)
    rest = scale
    for part in range(3):
        piece = rest.astype(jnp.bfloat16).astype(jnp.float32)
        rest = rest - piece
        riding = jnp.where(lane == scale_lane + part, piece, riding)
    ring_ref[:, pl.ds(share, lanes)] = riding.astype(jnp.bfloat16)


def combine_last(pick, slots, head, gain, sums):
    rows, width = head.shape
    share = slots.shape[1]
    return pl.pallas_call(
        last_kernel,
        out_shape=[
            jax.ShapeDtypeStruct((rows, width), jnp.bfloat16),
            jax.ShapeDtypeStruct((rows, share + lanes), jnp.bfloat16),
        ],
        compiler_params=pltpu.CompilerParams(vmem_limit_bytes=16 * MIB),
        cost_estimate=pl.CostEstimate(
            flops=4 * rows * slots.shape[0] * share,
            bytes_accessed=2 * (slots.size + 3 * rows * width),
            transcendentals=0,
        ),
        name="combine_last",
    )(pick, slots, head, gain, sums)


def stack_kernel(*refs):
    out_ref = refs[-1]
    rows = refs[0].shape[0]
    for place, ref in enumerate(refs[:-1]):
        out_ref[pl.ds(place * rows, rows), :] = ref[...]


def stack(blocks):
    rows, columns = blocks[0].shape
    return pl.pallas_call(
        stack_kernel,
        out_shape=jax.ShapeDtypeStruct((len(blocks) * rows, columns), jnp.bfloat16),
        compiler_params=pltpu.CompilerParams(vmem_limit_bytes=16 * MIB),
        name="stack_blocks",
    )(*blocks)


def ring_kernel(
    rows,
    factors,
    me_ref,
    weight_ref,
    own_ref,
    other_ref,
    sums_ref,
    scale_ref,
    balance_ref,
    held_ref,
):
    chips = own_ref.shape[0] // rows
    share = own_ref.shape[1] - lanes
    chip = lax.shift_right_logical(me_ref[0], 1)
    first = (me_ref[0] & 1) == 0
    for step in range(chips):
        own = own_ref[step * rows : (step + 1) * rows, :]
        other = other_ref[step * rows : (step + 1) * rows, :]
        source = lax.rem(chip - step + chips, chips)
        pair = jnp.concatenate([jnp.where(first, own, other), jnp.where(first, other, own)], axis=0)
        held_ref[pl.ds(pl.multiple_of(source * 2 * rows, 2 * rows), 2 * rows), :] = pair
    sums_ref[...] = lax.dot_general(
        weight_ref[:, pl.ds(weight_ref.shape[1] - share, share)],
        held_ref[:, pl.ds(0, share)],
        (((1,), (1,)), ((), ())),
        preferred_element_type=jnp.float32,
    )
    lane = lax.broadcasted_iota(jnp.int32, (8, lanes), 1)
    parts = (lane >= scale_lane) & (lane < scale_lane + 3)
    scale = lax.dot_general(
        jnp.where(parts, 1.0, 0.0).astype(jnp.bfloat16),
        held_ref[:, pl.ds(share, lanes)],
        (((1,), (1,)), ((), ())),
        preferred_element_type=jnp.float32,
    )
    scale_ref[...] = scale[0:1]
    riding = jnp.zeros((16, lanes), jnp.float32)
    for source in range(2 * chips):
        riding = riding + held_ref[pl.ds(source * rows, 16), pl.ds(share, lanes)].astype(jnp.float32)
    tokens_of, pairs_of, experts = factors
    usage = (riding[0:1] + riding[1:2] + riding[2:3]) / pairs_of
    shares = (riding[3:4] + riding[4:5] + riding[5:6]) / tokens_of
    product = jnp.where(lane[0:1] < int(experts), usage * shares, 0.0)
    balance_ref[...] = experts * jnp.sum(product, axis=1, keepdims=True)


def ring_project(me, weight_t, own, other, rows, factors):
    columns, width = weight_t.shape
    count, share = 2 * own.shape[0], own.shape[1] - lanes
    vmem = pl.BlockSpec(memory_space=pltpu.VMEM)
    return pl.pallas_call(
        lambda *refs: ring_kernel(rows, factors, *refs),
        in_specs=[pl.BlockSpec(memory_space=pltpu.SMEM), vmem, vmem, vmem],
        out_specs=[vmem, vmem, vmem],
        out_shape=[
            jax.ShapeDtypeStruct((columns, count), jnp.float32),
            jax.ShapeDtypeStruct((1, count), jnp.float32),
            jax.ShapeDtypeStruct((1, 1), jnp.float32),
        ],
        scratch_shapes=[pltpu.VMEM((count, own.shape[1]), jnp.bfloat16)],
        compiler_params=pltpu.CompilerParams(vmem_limit_bytes=24 * MIB),
        cost_estimate=pl.CostEstimate(
            flops=2 * count * share * columns,
            bytes_accessed=2 * (count * share + columns * (width + 2 * count)),
            transcendentals=0,
        ),
        name="ring_project",
    )(me, weight_t, own, other)


def project_kernel(weight_ref, rows_ref, sums_ref, scale_ref, out_ref):
    product = lax.dot_general(
        weight_ref[...],
        rows_ref[...],
        (((1,), (1,)), ((), ())),
        preferred_element_type=jnp.float32,
    )
    out_ref[...] = ((product + sums_ref[...]) * scale_ref[...]).astype(jnp.bfloat16)


def project(weight_t, gathered, sums, scale, steps=2):
    count, share = gathered.shape
    columns = weight_t.shape[0]
    block = count // steps
    return pl.pallas_call(
        project_kernel,
        grid=(steps,),
        in_specs=[
            pl.BlockSpec((columns, share), lambda i: (0, 0)),
            pl.BlockSpec((block, share), lambda i: (i, 0)),
            pl.BlockSpec((columns, block), lambda i: (0, i)),
            pl.BlockSpec((1, block), lambda i: (0, i)),
        ],
        out_specs=pl.BlockSpec((columns, block), lambda i: (0, i)),
        out_shape=jax.ShapeDtypeStruct((columns, count), jnp.bfloat16),
        compiler_params=pltpu.CompilerParams(vmem_limit_bytes=56 * MIB),
        cost_estimate=pl.CostEstimate(
            flops=2 * count * share * columns,
            bytes_accessed=2 * (count * share + columns * (share + 3 * count)),
            transcendentals=0,
        ),
        name="qkv_project",
    )(weight_t, gathered, sums, scale)


def on_device(
    residual, expert_hidden, down_weight, gates, routes, router_probs, norm_gain, qkv_weight
):
    experts = lax.axis_size("tensor")
    rows, width = residual.shape
    slot_count = expert_hidden.shape[1] // experts
    split = width * 3 // 4
    gain = norm_gain.reshape(1, width)
    weight = down_weight[0]

    def slots_of(outputs):
        return lax.all_to_all(
            outputs.reshape(experts, slot_count, -1),
            "tensor",
            split_axis=0,
            concat_axis=0,
            tiled=True,
        ).reshape(experts * slot_count, -1)

    head_slots = slots_of(expert_project(expert_hidden[0], weight, 0, split, 2))
    tail_outputs = expert_project(expert_hidden[0], weight, split, width - split, 1)
    tail_slots = slots_of(tail_outputs)
    pick, sums = pick_matrix(
        routes.T, gates.T, router_probs.T, tail_outputs, slot_count
    )
    depth = 16
    breadth = lax.axis_size("dp") // depth
    lines = [[x * depth + z for z in range(depth)] for x in range(breadth)]
    cross = [[x * depth + z for x in range(breadth)] for z in range(depth)]
    sums = lax.psum(sums, "dp", axis_index_groups=lines)
    head, scaled, sums = combine_first(pick, head_slots, residual, gain, sums)
    gathered = lax.all_gather(scaled, "tensor", axis=0, tiled=True)
    sums = lax.psum(sums, "dp", axis_index_groups=cross)
    fresh, riding = combine_last(pick, tail_slots, head, gain, sums)

    def moved(block, chips):
        pairs = [(i, (i + 2 * chips) % experts) for i in range(experts)]
        return lax.ppermute(block, "tensor", pairs)

    up_1, down_1 = moved(riding, 1), moved(riding, -1)
    up_2, down_2 = moved(riding, 2), moved(riding, -2)
    up_3, down_3 = moved(up_1, 2), moved(down_1, -2)
    up_4 = moved(up_2, 2)
    own = stack([riding, up_1, up_2, up_3, up_4, down_3, down_2, down_1])
    other = lax.ppermute(own, "tensor", [(i, i ^ 1) for i in range(experts)])
    total_tokens = rows * lax.axis_size("dp") * experts
    factors = (float(total_tokens), float(total_tokens * routes.shape[1]), float(experts))
    me = lax.axis_index("tensor").astype(jnp.int32).reshape(1)
    weight_t = qkv_weight.T
    part, scale, balance = ring_project(me, weight_t, own, other, rows, factors)
    projected = project(weight_t, gathered, part, scale).T
    return (fresh, projected, balance.reshape(()))


def solution(mesh):
    in_specs = (
        P(("dp", "tensor"), None),
        P(("dp", "tensor"), None, None),
        P("tensor", None, None),
        P(("dp", "tensor"), None),
        P(("dp", "tensor"), None),
        P(("dp", "tensor"), None),
        P(),
        P(None, "tensor"),
    )
    out_specs = (P(("dp", "tensor"), None), P("dp", "tensor"), P())
    return jax.shard_map(
        on_device, mesh=mesh, in_specs=in_specs, out_specs=out_specs, check_vma=False
    )
```

time: 150 us -> 160 us (1.067)
  waiting for transfers between devices: 28.9 us -> 35.3 us
  Pallas kernels: 15.7 us -> 20.2 us
  local copies, waits for them, and re-layouts: 6.46 us -> 3.51 us
  starting transfers between devices: 45.8 us -> 48.1 us
    all_to_all x1 -> x2, starting transfers between devices: 17.8 us -> 24 us  [slots_of(): lax.all_to_all(outputs.reshape(experts, slot_count, -1), 'tensor', split_...]
    all_to_all x1 -> x2, waiting for transfers between devices: 10.2 us -> 15.6 us  [slots_of(): lax.all_to_all(outputs.reshape(experts, slot_count, -1), 'tensor', split_...]
    ppermute x7, waiting for transfers between devices: 12.7 us -> 16.7 us  [moved(): return lax.ppermute(block, 'tensor', pairs)]
    ppermute x1, starting transfers between devices: 5.66 us -> 2.05 us  [on_device(): other = lax.ppermute(own, 'tensor', [(i, i ^ 1) for i in range(experts)])]
    all_gather x1, waiting for transfers between devices: 3.11 us -> 0.01 us  [on_device(): gathered = lax.all_gather(scaled, 'tensor', axis=0, tiled=True)]
    psum x1, blocking collectives: 31.9 us -> 29.4 us  [on_device(): sums = lax.psum(sums, 'dp', axis_index_groups=lines)]
    psum x1, blocking collectives: 6.6 us -> 9.05 us  [on_device(): sums = lax.psum(sums, 'dp', axis_index_groups=cross)]
    unnamed x21 -> x20, local copies, waits for them, and re-layouts: 5.79 us -> 3.51 us
  transfers between devices with their start and end apart: 10 -> 11, of which waited for: 7 -> 7; matrix products, arithmetic and copies ran while one was open for 4% -> 0% of each run, Pallas kernels for 2% -> 5%
where the time goes in v3:
time: 160 us
  starting transfers between devices  48.1 us (30%)
  blocking collectives  38.4 us (24%)
  waiting for transfers between devices  35.3 us (22%)
  Pallas kernels  20.2 us (13%)
  between operations  14.2 us (9%)
  local copies, waits for them, and re-layouts  3.51 us (2%)
    psum x1, blocking collectives, on_device(): sums = lax.psum(sums, 'dp', axis_index_groups=lines)  29.4 us
    all_to_all x2, starting transfers between devices, slots_of(): lax.all_to_all(outputs.reshape(experts, slot_count, -1), 'tensor', split_...  24 us
    ppermute x7, starting transfers between devices, moved(): return lax.ppermute(block, 'tensor', pairs)  22 us
    ppermute x7, waiting for transfers between devices, moved(): return lax.ppermute(block, 'tensor', pairs)  16.7 us
    all_to_all x2, waiting for transfers between devices, slots_of(): lax.all_to_all(outputs.reshape(experts, slot_count, -1), 'tensor', split_...  15.6 us
    psum x1, blocking collectives, on_device(): sums = lax.psum(sums, 'dp', axis_index_groups=cross)  9.05 us
    pallas_call x2, Pallas kernels, expert_project(): pl.pallas_call(expert_kernel, grid=(steps,), in_specs=[pl.BlockSpec((slot...  7.19 us
    pallas_call x1, Pallas kernels, project(): pl.pallas_call(project_kernel, grid=(steps,), in_specs=[pl.BlockSpec((col...  6.1 us
  transfers between devices with their start and end apart: 11, of which 7 were waited for; matrix products, arithmetic and copies ran while one was open for 0% of the time, Pallas kernels for 5%

profile of v3, /device:TPU:1, one launch (start us, length us, event | category | flops | bytes accessed | tf_op | source)
XLA Modules:
  0.0 159.6 jit_solution(723669405973959970)
XLA Ops:
  7.2 4.2 %expert_project.3 = bf16[256,3072]{1,0:T(8,128)(2,1)} custom-call(bf16[256,768]{1,0:T(8,128)(2,1)} %bitcast.26, bf16[768,4096]{1,0:T(8,128)(2,1)} %bitcast.23), custom_call_target="tpu_custom_call" | custom-call | flops 1207959552 | bytes 6684672 | tf_op jit(solution)/shard_map/expert_project/pallas_call | solution.py:23
  11.4 17.6 %all-to-all-start.1 = ((bf16[16,16,3072]{2,1,0:T(8,128)(2,1)}), bf16[16,16,3072]{2,1,0:T(8,128)(2,1)S(1)}, u32[]{:S(2)}, u32[]{:S(2)}) async-start(bf16[16,16,3072]{2,1,0:T(8,128)(2,1)} %bitcast.25), calls=%async_computation.1 | async-start | bytes 3145728 | tf_op jit(solution)/shard_map/all_to_all | solution.py:338
  29.1 0.0 all-gather.2.cloned.1.call-start
  29.2 2.9 %expert_project.2.refs_3_ = bf16[256,1024]{1,0:T(8,128)(2,1)} custom-call(bf16[256,768]{1,0:T(8,128)(2,1)} %bitcast.27, bf16[768,4096]{1,0:T(8,128)(2,1)} %bitcast.24), custom_call_target="tpu_custom_call" | custom-call | flops 402653184 | bytes 2490368 | tf_op jit(solution)/shard_map/expert_project/pallas_call | solution.py:23
  32.1 0.2 pick_matrix.1
  32.4 29.4 %psum.14.sums_ref = f32[2,16]{1,0:T(2,128)S(1)} all-reduce(f32[2,16]{1,0:T(2,128)S(1)} %get-tuple-element.14), channel_id=1, replica_groups={{0,16,32,48,64,80,96,112,128,144,160,176,192,208,224,240},{256,272,288,..., use_global_device_ids=true, to_apply=%region_0.0 | all-reduce | flops 32 | bytes 256 | tf_op jit(solution)/shard_map/psum | solution.py:356
  61.7 5.8 %all-to-all-done.1 = bf16[16,16,3072]{2,1,0:T(8,128)(2,1)S(1)} async-done(((bf16[16,16,3072]{2,1,0:T(8,128)(2,1)}), bf16[16,16,3072]{2,1,0:T(8,128)(2,1)S(1)}, u32[]{:S(2)}, u32[]{:S(2)}) %all-to-all-start.1) | async-done | bytes 1572896 | tf_op jit(solution)/shard_map/all_to_all | solution.py:338
  67.5 1.2 combine_first.1
  68.8 0.8 copy-done.2
  69.6 6.4 %all-to-all-start = ((bf16[16,16,1024]{2,1,0:T(8,128)(2,1)}), bf16[16,16,1024]{2,1,0:T(8,128)(2,1)S(1)}, u32[]{:S(2)}, u32[]{:S(2)}) async-start(bf16[16,16,1024]{2,1,0:T(8,128)(2,1)} %bitcast.5), calls=%async_computation | async-start | bytes 1048576 | tf_op jit(solution)/shard_map/all_to_all | solution.py:338
  76.0 9.0 %psum.15.sums_ref = f32[2,16]{1,0:T(2,128)S(1)} all-reduce(f32[2,16]{1,0:T(2,128)S(1)} %get-tuple-element.16), channel_id=1, replica_groups={{0,256,512,768},{16,272,528,784},{32,288,544,800},{48,304,560,816},{64,..., use_global_device_ids=true, to_apply=%region_1.0 | all-reduce | flops 32 | bytes 256 | tf_op jit(solution)/shard_map/psum | solution.py:359
  85.0 9.8 %all-to-all-done = bf16[16,16,1024]{2,1,0:T(8,128)(2,1)S(1)} async-done(((bf16[16,16,1024]{2,1,0:T(8,128)(2,1)}), bf16[16,16,1024]{2,1,0:T(8,128)(2,1)S(1)}, u32[]{:S(2)}, u32[]{:S(2)}) %all-to-all-start) | async-done | bytes 524320 | tf_op jit(solution)/shard_map/all_to_all | solution.py:338
  94.8 1.1 copy-done.3
  95.8 1.1 combine_last.1
  96.9 1.9 %collective-permute-start = (bf16[64,1152]{1,0:T(8,128)(2,1)S(1)}, bf16[64,1152]{1,0:T(8,128)(2,1)S(1)}, u32[]{:S(2)}, u32[]{:S(2)}) collective-permute-start(bf16[64,1152]{1,0:T(8,128)(2,1)S(1)} %get-tuple-element.19.refs_0_), channel_id=1, source_target_pairs={{0,2},{1,3},{2,4},{3,5},{4,6},{5,7},{6,8},{7,9},{8,10},{9,11},{10,... | collective-permute-start | bytes 442376 | tf_op jit(solution)/shard_map/ppermute | solution.py:364
  98.8 3.8 %collective-permute-start.1 = (bf16[64,1152]{1,0:T(8,128)(2,1)S(1)}, bf16[64,1152]{1,0:T(8,128)(2,1)S(1)}, u32[]{:S(2)}, u32[]{:S(2)}) collective-permute-start(bf16[64,1152]{1,0:T(8,128)(2,1)S(1)} %get-tuple-element.19.refs_0_), channel_id=1, source_target_pairs={{0,4},{1,5},{2,6},{3,7},{4,8},{5,9},{6,10},{7,11},{8,12},{9,13},{1... | collective-permute-start | bytes 442376 | tf_op jit(solution)/shard_map/ppermute | solution.py:364
  102.6 2.7 %collective-permute-start.4 = (bf16[64,1152]{1,0:T(8,128)(2,1)S(1)}, bf16[64,1152]{1,0:T(8,128)(2,1)S(1)}, u32[]{:S(2)}, u32[]{:S(2)}) collective-permute-start(bf16[64,1152]{1,0:T(8,128)(2,1)S(1)} %get-tuple-element.19.refs_0_), channel_id=1, source_target_pairs={{0,14},{1,15},{2,0},{3,1},{4,2},{5,3},{6,4},{7,5},{8,6},{9,7},{10,... | collective-permute-start | bytes 442376 | tf_op jit(solution)/shard_map/ppermute | solution.py:364
  105.3 4.3 %collective-permute-start.6 = (bf16[64,1152]{1,0:T(8,128)(2,1)S(1)}, bf16[64,1152]{1,0:T(8,128)(2,1)S(1)}, u32[]{:S(2)}, u32[]{:S(2)}) collective-permute-start(bf16[64,1152]{1,0:T(8,128)(2,1)S(1)} %get-tuple-element.19.refs_0_), channel_id=1, source_target_pairs={{0,12},{1,13},{2,14},{3,15},{4,0},{5,1},{6,2},{7,3},{8,4},{9,5},{1... | collective-permute-start | bytes 442376 | tf_op jit(solution)/shard_map/ppermute | solution.py:364
  109.6 0.7 collective-permute-done.refs_1_
  110.3 1.9 %collective-permute-start.2 = (bf16[64,1152]{1,0:T(8,128)(2,1)S(1)}, bf16[64,1152]{1,0:T(8,128)(2,1)S(1)}, u32[]{:S(2)}, u32[]{:S(2)}) collective-permute-start(bf16[64,1152]{1,0:T(8,128)(2,1)S(1)} %collective-permute-done.refs_1_), channel_id=1, source_target_pairs={{0,4},{1,5},{2,6},{3,7},{4,8},{5,9},{6,10},{7,11},{8,12},{9,13},{1... | collective-permute-start | bytes 442376 | tf_op jit(solution)/shard_map/ppermute | solution.py:364
  112.2 2.6 %collective-permute-done.1.refs_2_ = bf16[64,1152]{1,0:T(8,128)(2,1)S(1)} collective-permute-done((bf16[64,1152]{1,0:T(8,128)(2,1)S(1)}, bf16[64,1152]{1,0:T(8,128)(2,1)S(1)}, u32[]{:S(2)}, u32[]{:S(2)}) %collective-permute-start.1) | collective-permute-done | bytes 147488 | tf_op jit(solution)/shard_map/ppermute | solution.py:364
  114.9 2.7 %collective-permute-start.3 = (bf16[64,1152]{1,0:T(8,128)(2,1)S(1)}, bf16[64,1152]{1,0:T(8,128)(2,1)S(1)}, u32[]{:S(2)}, u32[]{:S(2)}) collective-permute-start(bf16[64,1152]{1,0:T(8,128)(2,1)S(1)} %collective-permute-done.1.refs_2_), channel_id=1, source_target_pairs={{0,4},{1,5},{2,6},{3,7},{4,8},{5,9},{6,10},{7,11},{8,12},{9,13},{1... | collective-permute-start | bytes 442376 | tf_op jit(solution)/shard_map/ppermute | solution.py:364
  117.6 4.6 %collective-permute-start.5 = (bf16[64,1152]{1,0:T(8,128)(2,1)S(1)}, bf16[64,1152]{1,0:T(8,128)(2,1)S(1)}, u32[]{:S(2)}, u32[]{:S(2)}) collective-permute-start(bf16[64,1152]{1,0:T(8,128)(2,1)S(1)} %collective-permute-done.4.refs_7_), channel_id=1, source_target_pairs={{0,12},{1,13},{2,14},{3,15},{4,0},{5,1},{6,2},{7,3},{8,4},{9,5},{1... | collective-permute-start | bytes 442376 | tf_op jit(solution)/shard_map/ppermute | solution.py:364
  122.3 4.1 %collective-permute-done.2.refs_3_ = bf16[64,1152]{1,0:T(8,128)(2,1)S(1)} collective-permute-done((bf16[64,1152]{1,0:T(8,128)(2,1)S(1)}, bf16[64,1152]{1,0:T(8,128)(2,1)S(1)}, u32[]{:S(2)}, u32[]{:S(2)}) %collective-permute-start.2) | collective-permute-done | bytes 147488 | tf_op jit(solution)/shard_map/ppermute | solution.py:364
  126.4 9.2 %collective-permute-done.3.refs_4_ = bf16[64,1152]{1,0:T(8,128)(2,1)S(1)} collective-permute-done((bf16[64,1152]{1,0:T(8,128)(2,1)S(1)}, bf16[64,1152]{1,0:T(8,128)(2,1)S(1)}, u32[]{:S(2)}, u32[]{:S(2)}) %collective-permute-start.3) | collective-permute-done | bytes 147488 | tf_op jit(solution)/shard_map/ppermute | solution.py:364
  135.6 1.1 stack_blocks.1.refs_2_
  136.7 2.1 %collective-permute-start.7 = (bf16[512,1152]{1,0:T(8,128)(2,1)}, bf16[512,1152]{1,0:T(8,128)(2,1)}, u32[]{:S(2)}, u32[]{:S(2)}) collective-permute-start(bf16[512,1152]{1,0:T(8,128)(2,1)} %stack_blocks.1.refs_2_), channel_id=1, source_target_pairs={{0,1},{1,0},{2,3},{3,2},{4,5},{5,4},{6,7},{7,6},{8,9},{9,8},{10,11... | collective-permute-start | bytes 3538952 | tf_op jit(solution)/shard_map/ppermute | solution.py:371
  138.7 3.0 %collective-permute-done.7.refs_3_ = bf16[512,1152]{1,0:T(8,128)(2,1)} collective-permute-done((bf16[512,1152]{1,0:T(8,128)(2,1)}, bf16[512,1152]{1,0:T(8,128)(2,1)}, u32[]{:S(2)}, u32[]{:S(2)}) %collective-permute-start.7) | collective-permute-done | bytes 1179680 | tf_op jit(solution)/shard_map/ppermute | solution.py:371
  141.8 3.2 %ring_project.1 = (f32[320,1024]{1,0:T(8,128)S(1)}, f32[1,1024]{1,0:T(1,128)S(1)}, f32[1,1]{1,0:T(1,128)}) custom-call(s32[1]{0:T(128)} %bitcast.11.refs_0_, bf16[320,4096]{1,0:T(8,128)(2,1)S(1)} %bitcast.15, bf16[512,1152]{1,0:T(8,128)(2,1)} %stack_blocks.1.refs_2_, bf16[512,1152]{1,0:T(8,128)(2,1)} %collective-permute-done.7.refs_3_), custom_call_target="tpu_custom_call" | custom-call | flops 671088640 | bytes 6029312 | tf_op jit(solution)/shard_map/ring_project/pallas_call | solution.py:272
  145.0 1.0 copy-done.1
  146.0 0.6 copy-done.7
  146.6 6.1 %qkv_project.1 = bf16[320,1024]{1,0:T(8,128)(2,1)} custom-call(bf16[320,4096]{1,0:T(8,128)(2,1)} %bitcast.14, bf16[1024,3072]{1,0:T(8,128)(2,1)} %all-gather.2.cloned.1.call-done.rows_ref, f32[320,1024]{1,0:T(8,128)} %copy-done.1, f32[1,1024]{1,0:T(1,128)} %copy-done.7), custom_call_target="tpu_custom_call" | custom-call | flops 2013265920 | bytes 10223616 | tf_op jit(solution)/shard_map/qkv_project/pallas_call | solution.py:306
  (21 shorter events, 0.1 us)
Async XLA Ops:
  11.4 56.1 %all-to-all-start.1 = ((bf16[16,16,3072]{2,1,0:T(8,128)(2,1)}), bf16[16,16,3072]{2,1,0:T(8,128)(2,1)S(1)}, u32[]{:S(2)}, u32[]{:S(2)}) async-start(bf16[16,16,3072]{2,1,0:T(8,128)(2,1)} %bitcast.25), calls=%async_computation.1 | async-start | bytes 3145728 | tf_op jit(solution)/shard_map/all_to_all | solution.py:338
  29.1 3.1 %copy-start.6 = (f32[64,16]{0,1:T(8,128)S(1)}, f32[64,16]{0,1:T(8,128)}, u32[]{:S(2)}) copy-start(f32[64,16]{0,1:T(8,128)} %param.13) | copy-start | bytes 12292
  29.1 3.0 %copy-start.8 = (s32[64,2]{0,1:T(2,128)S(1)}, s32[64,2]{0,1:T(2,128)}, u32[]{:S(2)}) copy-start(s32[64,2]{0,1:T(2,128)} %param.12) | copy-start | bytes 1540
  29.1 3.0 %copy-start.9 = (f32[64,2]{0,1:T(2,128)S(1)}, f32[64,2]{0,1:T(2,128)}, u32[]{:S(2)}) copy-start(f32[64,2]{0,1:T(2,128)} %param.11) | copy-start | bytes 1540
  29.1 38.4 %copy-start.4 = (bf16[64,4096]{1,0:T(8,128)(2,1)S(1)}, bf16[64,4096]{1,0:T(8,128)(2,1)}, u32[]{:S(2)}) copy-start(bf16[64,4096]{1,0:T(8,128)(2,1)} %residual_ref.1) | copy-start | bytes 1572868
  29.1 38.4 %copy-start.5 = (f32[4096]{0:T(1024)S(1)}, f32[4096]{0:T(1024)}, u32[]{:S(2)}) copy-start(f32[4096]{0:T(1024)} %param.14) | copy-start | bytes 49156
  29.1 117.5 %all-gather.2.cloned.1.call-start = ((), (), s32[]{:S(2)}) async-start(), calls=%async_computation.2 | async-start | bytes 6684672 | tf_op jit(solution)/shard_map/all_gather | solution.py:358
  68.8 0.8 copy-start.2
  69.6 25.2 %all-to-all-start = ((bf16[16,16,1024]{2,1,0:T(8,128)(2,1)}), bf16[16,16,1024]{2,1,0:T(8,128)(2,1)S(1)}, u32[]{:S(2)}, u32[]{:S(2)}) async-start(bf16[16,16,1024]{2,1,0:T(8,128)(2,1)} %bitcast.5), calls=%async_computation | async-start | bytes 1048576 | tf_op jit(solution)/shard_map/all_to_all | solution.py:338
  94.8 1.1 copy-start.3
  95.8 45.9 %copy-start = (bf16[4096,320]{0,1:T(8,128)(2,1)S(1)}, bf16[4096,320]{0,1:T(8,128)(2,1)}, u32[]{:S(2)}) copy-start(bf16[4096,320]{0,1:T(8,128)(2,1)} %param.15) | copy-start | bytes 7864324
  96.9 13.4 %collective-permute-start = (bf16[64,1152]{1,0:T(8,128)(2,1)S(1)}, bf16[64,1152]{1,0:T(8,128)(2,1)S(1)}, u32[]{:S(2)}, u32[]{:S(2)}) collective-permute-start(bf16[64,1152]{1,0:T(8,128)(2,1)S(1)} %get-tuple-element.19.refs_0_), channel_id=1, source_target_pairs={{0,2},{1,3},{2,4},{3,5},{4,6},{5,7},{6,8},{7,9},{8,10},{9,11},{10,... | collective-permute-start | bytes 442376 | tf_op jit(solution)/shard_map/ppermute | solution.py:364
  98.8 16.1 %collective-permute-start.1 = (bf16[64,1152]{1,0:T(8,128)(2,1)S(1)}, bf16[64,1152]{1,0:T(8,128)(2,1)S(1)}, u32[]{:S(2)}, u32[]{:S(2)}) collective-permute-start(bf16[64,1152]{1,0:T(8,128)(2,1)S(1)} %get-tuple-element.19.refs_0_), channel_id=1, source_target_pairs={{0,4},{1,5},{2,6},{3,7},{4,8},{5,9},{6,10},{7,11},{8,12},{9,13},{1... | collective-permute-start | bytes 442376 | tf_op jit(solution)/shard_map/ppermute | solution.py:364
  102.6 15.0 %collective-permute-start.4 = (bf16[64,1152]{1,0:T(8,128)(2,1)S(1)}, bf16[64,1152]{1,0:T(8,128)(2,1)S(1)}, u32[]{:S(2)}, u32[]{:S(2)}) collective-permute-start(bf16[64,1152]{1,0:T(8,128)(2,1)S(1)} %get-tuple-element.19.refs_0_), channel_id=1, source_target_pairs={{0,14},{1,15},{2,0},{3,1},{4,2},{5,3},{6,4},{7,5},{8,6},{9,7},{10,... | collective-permute-start | bytes 442376 | tf_op jit(solution)/shard_map/ppermute | solution.py:364
  105.3 17.0 %collective-permute-start.6 = (bf16[64,1152]{1,0:T(8,128)(2,1)S(1)}, bf16[64,1152]{1,0:T(8,128)(2,1)S(1)}, u32[]{:S(2)}, u32[]{:S(2)}) collective-permute-start(bf16[64,1152]{1,0:T(8,128)(2,1)S(1)} %get-tuple-element.19.refs_0_), channel_id=1, source_target_pairs={{0,12},{1,13},{2,14},{3,15},{4,0},{5,1},{6,2},{7,3},{8,4},{9,5},{1... | collective-permute-start | bytes 442376 | tf_op jit(solution)/shard_map/ppermute | solution.py:364
  110.3 16.1 %collective-permute-start.2 = (bf16[64,1152]{1,0:T(8,128)(2,1)S(1)}, bf16[64,1152]{1,0:T(8,128)(2,1)S(1)}, u32[]{:S(2)}, u32[]{:S(2)}) collective-permute-start(bf16[64,1152]{1,0:T(8,128)(2,1)S(1)} %collective-permute-done.refs_1_), channel_id=1, source_target_pairs={{0,4},{1,5},{2,6},{3,7},{4,8},{5,9},{6,10},{7,11},{8,12},{9,13},{1... | collective-permute-start | bytes 442376 | tf_op jit(solution)/shard_map/ppermute | solution.py:364
  114.9 20.7 %collective-permute-start.3 = (bf16[64,1152]{1,0:T(8,128)(2,1)S(1)}, bf16[64,1152]{1,0:T(8,128)(2,1)S(1)}, u32[]{:S(2)}, u32[]{:S(2)}) collective-permute-start(bf16[64,1152]{1,0:T(8,128)(2,1)S(1)} %collective-permute-done.1.refs_2_), channel_id=1, source_target_pairs={{0,4},{1,5},{2,6},{3,7},{4,8},{5,9},{6,10},{7,11},{8,12},{9,13},{1... | collective-permute-start | bytes 442376 | tf_op jit(solution)/shard_map/ppermute | solution.py:364
  117.6 17.9 %collective-permute-start.5 = (bf16[64,1152]{1,0:T(8,128)(2,1)S(1)}, bf16[64,1152]{1,0:T(8,128)(2,1)S(1)}, u32[]{:S(2)}, u32[]{:S(2)}) collective-permute-start(bf16[64,1152]{1,0:T(8,128)(2,1)S(1)} %collective-permute-done.4.refs_7_), channel_id=1, source_target_pairs={{0,12},{1,13},{2,14},{3,15},{4,0},{5,1},{6,2},{7,3},{8,4},{9,5},{1... | collective-permute-start | bytes 442376 | tf_op jit(solution)/shard_map/ppermute | solution.py:364
  136.7 5.1 %collective-permute-start.7 = (bf16[512,1152]{1,0:T(8,128)(2,1)}, bf16[512,1152]{1,0:T(8,128)(2,1)}, u32[]{:S(2)}, u32[]{:S(2)}) collective-permute-start(bf16[512,1152]{1,0:T(8,128)(2,1)} %stack_blocks.1.refs_2_), channel_id=1, source_target_pairs={{0,1},{1,0},{2,3},{3,2},{4,5},{5,4},{6,7},{7,6},{8,9},{9,8},{10,11... | collective-permute-start | bytes 3538952 | tf_op jit(solution)/shard_map/ppermute | solution.py:371
  145.0 1.0 copy-start.1
  146.0 0.6 copy-start.7
Sparse Core Ops, SparseCore 0:
  69.7 74.9 all-gather.1

commit v4 on v2

--- a/solution.py
+++ b/solution.py
@@ -169,6 +169,23 @@
     )(pick, slots, residual, gain, counts, shares)
 
 
+def stack_kernel(*refs):
+    out_ref = refs[-1]
+    rows = refs[0].shape[0]
+    for place, ref in enumerate(refs[:-1]):
+        out_ref[pl.ds(place * rows, rows), :] = ref[...]
+
+
+def stack(blocks):
+    rows, columns = blocks[0].shape
+    return pl.pallas_call(
+        stack_kernel,
+        out_shape=jax.ShapeDtypeStruct((len(blocks) * rows, columns), jnp.bfloat16),
+        compiler_params=pltpu.CompilerParams(vmem_limit_bytes=16 * MIB),
+        name="stack_blocks",
+    )(*blocks)
+
+
 def ring_kernel(
     rows, factors, me_ref, weight_ref, own_ref, other_ref, sums_ref, balance_ref, held_ref
 ):
@@ -260,7 +277,7 @@
     experts = lax.axis_size("tensor")
     rows, width = residual.shape
     slot_count = expert_hidden.shape[1] // experts
-    split = width * 3 // 4
+    split = width * 5 // 8
     expert_out = expert_project(expert_hidden[0], down_weight[0])
     returned = lax.all_to_all(
         expert_out.reshape(experts, slot_count, width),
@@ -288,7 +305,7 @@
         ups.append(lax.ppermute(ups[-1], "tensor", up))
         if step < chips // 2 - 1:
             downs.append(lax.ppermute(downs[-1], "tensor", down))
-    own = jnp.concatenate(ups + downs[:0:-1], axis=0)
+    own = stack(ups + downs[:0:-1])
     other = lax.ppermute(own, "tensor", [(i, i ^ 1) for i in range(experts)])
     total_tokens = rows * lax.axis_size("dp") * experts
     factors = (float(total_tokens), float(total_tokens * routes.shape[1]), float(experts))

time: 150 us -> 155 us (1.033)
  waiting for transfers between devices: 28.9 us -> 36.1 us
  local copies, waits for them, and re-layouts: 6.46 us -> 1.12 us
  starting transfers between devices: 45.8 us -> 47.7 us
    ppermute x4, waiting for transfers between devices: 10.9 us -> 19.8 us  [on_device(): ups.append(lax.ppermute(ups[-1], 'tensor', up))]
    unnamed x21 -> x14, local copies, waits for them, and re-layouts: 5.79 us -> 1.12 us
    all_gather x1, waiting for transfers between devices: 3.11 us -> 0.01 us  [on_device(): gathered = lax.all_gather(normed, 'tensor', axis=0, tiled=True)]
    ppermute x1, starting transfers between devices: 5.66 us -> 7.9 us  [on_device(): other = lax.ppermute(own, 'tensor', [(i, i ^ 1) for i in range(experts)])]
  transfers between devices with their start and end apart: 10 -> 10, of which waited for: 7 -> 8; matrix products, arithmetic and copies ran while one was open for 4% -> 0% of each run, Pallas kernels for 2% -> 4%
where the time goes in v4:
time: 155 us
  starting transfers between devices  47.7 us (31%)
  blocking collectives  38.5 us (25%)
  waiting for transfers between devices  36.1 us (23%)
  Pallas kernels  17.1 us (11%)
  between operations  14.2 us (9%)
    psum x1, blocking collectives, on_device(): sums = lax.psum(sums, 'dp', axis_index_groups=lines)  31.9 us
    ppermute x4, waiting for transfers between devices, on_device(): ups.append(lax.ppermute(ups[-1], 'tensor', up))  19.8 us
    all_to_all x1, starting transfers between devices, on_device(): lax.all_to_all(expert_out.reshape(experts, slot_count, width), 'tensor',...  17.8 us
    ppermute x3, starting transfers between devices, on_device(): downs.append(lax.ppermute(downs[-1], 'tensor', down))  14.2 us
    all_to_all x1, waiting for transfers between devices, on_device(): lax.all_to_all(expert_out.reshape(experts, slot_count, width), 'tensor',...  10.2 us
    ppermute x1, starting transfers between devices, on_device(): other = lax.ppermute(own, 'tensor', [(i, i ^ 1) for i in range(experts)])  7.9 us
    ppermute x4, starting transfers between devices, on_device(): ups.append(lax.ppermute(ups[-1], 'tensor', up))  7.78 us
    psum x1, blocking collectives, on_device(): sums = lax.psum((counts, shares), 'dp', axis_index_groups=cross)  6.6 us
  transfers between devices with their start and end apart: 10, of which 8 were waited for; matrix products, arithmetic and copies ran while one was open for 0% of the time, Pallas kernels for 4%

profile of v4, /device:TPU:1, one launch (start us, length us, event | category | flops | bytes accessed | tf_op | source)
XLA Modules:
  0.0 154.8 jit_solution(11150614452710572329)
XLA Ops:
  7.2 5.0 %expert_project.1 = bf16[256,4096]{1,0:T(8,128)(2,1)} custom-call(bf16[256,768]{1,0:T(8,128)(2,1)} %bitcast.22, bf16[768,4096]{1,0:T(8,128)(2,1)} %bitcast.20), custom_call_target="tpu_custom_call" | custom-call | flops 1610612736 | bytes 8781824 | tf_op jit(solution)/shard_map/expert_project/pallas_call | solution.py:32
  12.1 0.0 copy-start.2
  12.1 0.0 copy-start.3
  12.2 17.8 %all-to-all-start = ((bf16[16,16,4096]{2,1,0:T(8,128)(2,1)}), bf16[16,16,4096]{2,1,0:T(8,128)(2,1)S(1)}, u32[]{:S(2)}, u32[]{:S(2)}) async-start(bf16[16,16,4096]{2,1,0:T(8,128)(2,1)} %bitcast.19), calls=%async_computation | async-start | bytes 4194304 | tf_op jit(solution)/shard_map/all_to_all | solution.py:282
  30.0 0.0 all-gather.2.cloned.1.call-start
  30.0 0.2 pick_matrix.1
  30.3 6.6 %all-reduce.1 = (f32[1,16]{1,0:T(1,128)S(1)}, f32[1,16]{1,0:T(1,128)S(1)}) all-reduce(f32[1,16]{1,0:T(1,128)S(1)} %get-tuple-element.12, f32[1,16]{1,0:T(1,128)S(1)} %get-tuple-element.13), channel_id=1, replica_groups={{0,256,512,768},{16,272,528,784},{32,288,544,800},{48,304,560,816},{64,..., use_global_device_ids=true, to_apply=%region_0.0 | all-reduce | flops 32 | bytes 256 | tf_op jit(solution)/shard_map/psum | solution.py:294
  36.9 31.9 %all-reduce = (f32[1,16]{1,0:T(1,128)S(1)}, f32[1,16]{1,0:T(1,128)S(1)}) all-reduce(f32[1,16]{1,0:T(1,128)S(1)} %get-tuple-element.21, f32[1,16]{1,0:T(1,128)S(1)} %get-tuple-element.22), channel_id=1, replica_groups={{0,16,32,48,64,80,96,112,128,144,160,176,192,208,224,240},{256,272,288,..., use_global_device_ids=true, to_apply=%region_1.0 | all-reduce | flops 32 | bytes 256 | tf_op jit(solution)/shard_map/psum | solution.py:295
  68.8 10.2 %all-to-all-done = bf16[16,16,4096]{2,1,0:T(8,128)(2,1)S(1)} async-done(((bf16[16,16,4096]{2,1,0:T(8,128)(2,1)}), bf16[16,16,4096]{2,1,0:T(8,128)(2,1)S(1)}, u32[]{:S(2)}, u32[]{:S(2)}) %all-to-all-start) | async-done | bytes 2097184 | tf_op jit(solution)/shard_map/all_to_all | solution.py:282
  78.9 0.0 copy-done.3
  79.0 1.4 combine_and_norm.1
  80.4 0.0 all-gather.2.cloned.1.call-update
  80.4 2.1 %collective-permute-start = (bf16[64,1664]{1,0:T(8,128)(2,1)S(1)}, bf16[64,1664]{1,0:T(8,128)(2,1)S(1)}, u32[]{:S(2)}, u32[]{:S(2)}) collective-permute-start(bf16[64,1664]{1,0:T(8,128)(2,1)S(1)} %get-tuple-element.16.refs_0_), channel_id=1, source_target_pairs={{0,2},{1,3},{2,4},{3,5},{4,6},{5,7},{6,8},{7,9},{8,10},{9,11},{10,... | collective-permute-start | bytes 638984 | tf_op jit(solution)/shard_map/ppermute | solution.py:305
  82.4 4.6 %collective-permute-start.4 = (bf16[64,1664]{1,0:T(8,128)(2,1)S(1)}, bf16[64,1664]{1,0:T(8,128)(2,1)S(1)}, u32[]{:S(2)}, u32[]{:S(2)}) collective-permute-start(bf16[64,1664]{1,0:T(8,128)(2,1)S(1)} %get-tuple-element.16.refs_0_), channel_id=1, source_target_pairs={{0,14},{1,15},{2,0},{3,1},{4,2},{5,3},{6,4},{7,5},{8,6},{9,7},{10,... | collective-permute-start | bytes 638984 | tf_op jit(solution)/shard_map/ppermute | solution.py:307
  87.0 3.0 %collective-permute-done.refs_1_ = bf16[64,1664]{1,0:T(8,128)(2,1)S(1)} collective-permute-done((bf16[64,1664]{1,0:T(8,128)(2,1)S(1)}, bf16[64,1664]{1,0:T(8,128)(2,1)S(1)}, u32[]{:S(2)}, u32[]{:S(2)}) %collective-permute-start) | collective-permute-done | bytes 213024 | tf_op jit(solution)/shard_map/ppermute | solution.py:305
  90.1 1.9 %collective-permute-start.1 = (bf16[64,1664]{1,0:T(8,128)(2,1)S(1)}, bf16[64,1664]{1,0:T(8,128)(2,1)S(1)}, u32[]{:S(2)}, u32[]{:S(2)}) collective-permute-start(bf16[64,1664]{1,0:T(8,128)(2,1)S(1)} %collective-permute-done.refs_1_), channel_id=1, source_target_pairs={{0,2},{1,3},{2,4},{3,5},{4,6},{5,7},{6,8},{7,9},{8,10},{9,11},{10,... | collective-permute-start | bytes 638984 | tf_op jit(solution)/shard_map/ppermute | solution.py:305
  92.0 0.0 collective-permute-done.4.refs_7_
  92.0 4.6 %collective-permute-start.5 = (bf16[64,1664]{1,0:T(8,128)(2,1)S(1)}, bf16[64,1664]{1,0:T(8,128)(2,1)S(1)}, u32[]{:S(2)}, u32[]{:S(2)}) collective-permute-start(bf16[64,1664]{1,0:T(8,128)(2,1)S(1)} %collective-permute-done.4.refs_7_), channel_id=1, source_target_pairs={{0,14},{1,15},{2,0},{3,1},{4,2},{5,3},{6,4},{7,5},{8,6},{9,7},{10,... | collective-permute-start | bytes 638984 | tf_op jit(solution)/shard_map/ppermute | solution.py:307
  96.6 2.1 %collective-permute-done.1.refs_2_ = bf16[64,1664]{1,0:T(8,128)(2,1)S(1)} collective-permute-done((bf16[64,1664]{1,0:T(8,128)(2,1)S(1)}, bf16[64,1664]{1,0:T(8,128)(2,1)S(1)}, u32[]{:S(2)}, u32[]{:S(2)}) %collective-permute-start.1) | collective-permute-done | bytes 213024 | tf_op jit(solution)/shard_map/ppermute | solution.py:305
  98.7 1.9 %collective-permute-start.2 = (bf16[64,1664]{1,0:T(8,128)(2,1)S(1)}, bf16[64,1664]{1,0:T(8,128)(2,1)S(1)}, u32[]{:S(2)}, u32[]{:S(2)}) collective-permute-start(bf16[64,1664]{1,0:T(8,128)(2,1)S(1)} %collective-permute-done.1.refs_2_), channel_id=1, source_target_pairs={{0,2},{1,3},{2,4},{3,5},{4,6},{5,7},{6,8},{7,9},{8,10},{9,11},{10,... | collective-permute-start | bytes 638984 | tf_op jit(solution)/shard_map/ppermute | solution.py:305
  100.6 1.2 collective-permute-done.5.refs_6_
  101.8 5.1 %collective-permute-start.6 = (bf16[64,1664]{1,0:T(8,128)(2,1)S(1)}, bf16[64,1664]{1,0:T(8,128)(2,1)S(1)}, u32[]{:S(2)}, u32[]{:S(2)}) collective-permute-start(bf16[64,1664]{1,0:T(8,128)(2,1)S(1)} %collective-permute-done.5.refs_6_), channel_id=1, source_target_pairs={{0,14},{1,15},{2,0},{3,1},{4,2},{5,3},{6,4},{7,5},{8,6},{9,7},{10,... | collective-permute-start | bytes 638984 | tf_op jit(solution)/shard_map/ppermute | solution.py:307
  106.9 4.7 %collective-permute-done.2.refs_3_ = bf16[64,1664]{1,0:T(8,128)(2,1)S(1)} collective-permute-done((bf16[64,1664]{1,0:T(8,128)(2,1)S(1)}, bf16[64,1664]{1,0:T(8,128)(2,1)S(1)}, u32[]{:S(2)}, u32[]{:S(2)}) %collective-permute-start.2) | collective-permute-done | bytes 213024 | tf_op jit(solution)/shard_map/ppermute | solution.py:305
  111.6 1.9 %collective-permute-start.3 = (bf16[64,1664]{1,0:T(8,128)(2,1)S(1)}, bf16[64,1664]{1,0:T(8,128)(2,1)S(1)}, u32[]{:S(2)}, u32[]{:S(2)}) collective-permute-start(bf16[64,1664]{1,0:T(8,128)(2,1)S(1)} %collective-permute-done.2.refs_3_), channel_id=1, source_target_pairs={{0,2},{1,3},{2,4},{3,5},{4,6},{5,7},{6,8},{7,9},{8,10},{9,11},{10,... | collective-permute-start | bytes 638984 | tf_op jit(solution)/shard_map/ppermute | solution.py:305
  113.5 1.3 collective-permute-done.6.refs_5_
  114.8 9.9 %collective-permute-done.3.refs_4_ = bf16[64,1664]{1,0:T(8,128)(2,1)S(1)} collective-permute-done((bf16[64,1664]{1,0:T(8,128)(2,1)S(1)}, bf16[64,1664]{1,0:T(8,128)(2,1)S(1)}, u32[]{:S(2)}, u32[]{:S(2)}) %collective-permute-start.3) | collective-permute-done | bytes 213024 | tf_op jit(solution)/shard_map/ppermute | solution.py:305
  124.7 1.3 stack_blocks.1.refs_2_
  126.1 7.9 %collective-permute-start.7 = (bf16[512,1664]{1,0:T(8,128)(2,1)}, bf16[512,1664]{1,0:T(8,128)(2,1)}, u32[]{:S(2)}, u32[]{:S(2)}) collective-permute-start(bf16[512,1664]{1,0:T(8,128)(2,1)} %stack_blocks.1.refs_2_), channel_id=1, source_target_pairs={{0,1},{1,0},{2,3},{3,2},{4,5},{5,4},{6,7},{7,6},{8,9},{9,8},{10,11... | collective-permute-start | bytes 5111816 | tf_op jit(solution)/shard_map/ppermute | solution.py:309
  134.0 3.7 %collective-permute-done.7.refs_3_ = bf16[512,1664]{1,0:T(8,128)(2,1)} collective-permute-done((bf16[512,1664]{1,0:T(8,128)(2,1)}, bf16[512,1664]{1,0:T(8,128)(2,1)}, u32[]{:S(2)}, u32[]{:S(2)}) %collective-permute-start.7) | collective-permute-done | bytes 1703968 | tf_op jit(solution)/shard_map/ppermute | solution.py:309
  137.6 3.9 %ring_project.1 = (f32[320,1024]{1,0:T(8,128)S(1)}, f32[1,1]{1,0:T(1,128)}) custom-call(s32[1]{0:T(128)} %bitcast.9.refs_0_, bf16[320,4096]{1,0:T(8,128)(2,1)S(1)} %bitcast.13, bf16[512,1664]{1,0:T(8,128)(2,1)} %stack_blocks.1.refs_2_, bf16[512,1664]{1,0:T(8,128)(2,1)} %collective-permute-done.7.refs_3_), custom_call_target="tpu_custom_call" | custom-call | flops 1006632960 | bytes 7077888 | tf_op jit(solution)/shard_map/ring_project/pallas_call | solution.py:221
  141.6 1.1 copy-done.1
  142.7 5.3 %qkv_project.1 = bf16[320,1024]{1,0:T(8,128)(2,1)} custom-call(bf16[320,4096]{1,0:T(8,128)(2,1)} %bitcast.12, bf16[1024,2560]{1,0:T(8,128)(2,1)} %all-gather.2.cloned.1.call-done.rows_ref, f32[320,1024]{1,0:T(8,128)} %copy-done.1), custom_call_target="tpu_custom_call" | custom-call | flops 1677721600 | bytes 8847360 | tf_op jit(solution)/shard_map/qkv_project/pallas_call | solution.py:254
  (11 shorter events, 0.0 us)
Async XLA Ops:
  12.1 17.9 %copy-start.4 = (f32[64,16]{0,1:T(8,128)S(1)}, f32[64,16]{0,1:T(8,128)}, u32[]{:S(2)}) copy-start(f32[64,16]{0,1:T(8,128)} %param.13) | copy-start | bytes 12292
  12.1 17.9 %copy-start.5 = (s32[64,2]{0,1:T(2,128)S(1)}, s32[64,2]{0,1:T(2,128)}, u32[]{:S(2)}) copy-start(s32[64,2]{0,1:T(2,128)} %param.12) | copy-start | bytes 1540
  12.1 17.9 %copy-start.6 = (f32[64,2]{0,1:T(2,128)S(1)}, f32[64,2]{0,1:T(2,128)}, u32[]{:S(2)}) copy-start(f32[64,2]{0,1:T(2,128)} %param.11) | copy-start | bytes 1540
  12.1 66.8 %copy-start.2 = (bf16[64,4096]{1,0:T(8,128)(2,1)S(1)}, bf16[64,4096]{1,0:T(8,128)(2,1)}, u32[]{:S(2)}) copy-start(bf16[64,4096]{1,0:T(8,128)(2,1)} %residual_ref.1) | copy-start | bytes 1572868
  12.1 66.8 %copy-start.3 = (f32[4096]{0:T(1024)S(1)}, f32[4096]{0:T(1024)}, u32[]{:S(2)}) copy-start(f32[4096]{0:T(1024)} %param.14) | copy-start | bytes 49156
  12.2 66.8 %all-to-all-start = ((bf16[16,16,4096]{2,1,0:T(8,128)(2,1)}), bf16[16,16,4096]{2,1,0:T(8,128)(2,1)S(1)}, u32[]{:S(2)}, u32[]{:S(2)}) async-start(bf16[16,16,4096]{2,1,0:T(8,128)(2,1)} %bitcast.19), calls=%async_computation | async-start | bytes 4194304 | tf_op jit(solution)/shard_map/all_to_all | solution.py:282
  30.0 112.7 %all-gather.2.cloned.1.call-start = ((), (), s32[]{:S(2)}) async-start(), calls=%async_computation.1 | async-start | bytes 5570560 | tf_op jit(solution)/shard_map/all_gather | solution.py:299
  80.4 57.3 %copy-start = (bf16[4096,320]{0,1:T(8,128)(2,1)S(1)}, bf16[4096,320]{0,1:T(8,128)(2,1)}, u32[]{:S(2)}) copy-start(bf16[4096,320]{0,1:T(8,128)(2,1)} %param.15) | copy-start | bytes 7864324
  80.4 9.7 %collective-permute-start = (bf16[64,1664]{1,0:T(8,128)(2,1)S(1)}, bf16[64,1664]{1,0:T(8,128)(2,1)S(1)}, u32[]{:S(2)}, u32[]{:S(2)}) collective-permute-start(bf16[64,1664]{1,0:T(8,128)(2,1)S(1)} %get-tuple-element.16.refs_0_), channel_id=1, source_target_pairs={{0,2},{1,3},{2,4},{3,5},{4,6},{5,7},{6,8},{7,9},{8,10},{9,11},{10,... | collective-permute-start | bytes 638984 | tf_op jit(solution)/shard_map/ppermute | solution.py:305
  82.4 9.5 %collective-permute-start.4 = (bf16[64,1664]{1,0:T(8,128)(2,1)S(1)}, bf16[64,1664]{1,0:T(8,128)(2,1)S(1)}, u32[]{:S(2)}, u32[]{:S(2)}) collective-permute-start(bf16[64,1664]{1,0:T(8,128)(2,1)S(1)} %get-tuple-element.16.refs_0_), channel_id=1, source_target_pairs={{0,14},{1,15},{2,0},{3,1},{4,2},{5,3},{6,4},{7,5},{8,6},{9,7},{10,... | collective-permute-start | bytes 638984 | tf_op jit(solution)/shard_map/ppermute | solution.py:307
  90.1 8.6 %collective-permute-start.1 = (bf16[64,1664]{1,0:T(8,128)(2,1)S(1)}, bf16[64,1664]{1,0:T(8,128)(2,1)S(1)}, u32[]{:S(2)}, u32[]{:S(2)}) collective-permute-start(bf16[64,1664]{1,0:T(8,128)(2,1)S(1)} %collective-permute-done.refs_1_), channel_id=1, source_target_pairs={{0,2},{1,3},{2,4},{3,5},{4,6},{5,7},{6,8},{7,9},{8,10},{9,11},{10,... | collective-permute-start | bytes 638984 | tf_op jit(solution)/shard_map/ppermute | solution.py:305
  92.0 9.8 %collective-permute-start.5 = (bf16[64,1664]{1,0:T(8,128)(2,1)S(1)}, bf16[64,1664]{1,0:T(8,128)(2,1)S(1)}, u32[]{:S(2)}, u32[]{:S(2)}) collective-permute-start(bf16[64,1664]{1,0:T(8,128)(2,1)S(1)} %collective-permute-done.4.refs_7_), channel_id=1, source_target_pairs={{0,14},{1,15},{2,0},{3,1},{4,2},{5,3},{6,4},{7,5},{8,6},{9,7},{10,... | collective-permute-start | bytes 638984 | tf_op jit(solution)/shard_map/ppermute | solution.py:307
  98.7 13.0 %collective-permute-start.2 = (bf16[64,1664]{1,0:T(8,128)(2,1)S(1)}, bf16[64,1664]{1,0:T(8,128)(2,1)S(1)}, u32[]{:S(2)}, u32[]{:S(2)}) collective-permute-start(bf16[64,1664]{1,0:T(8,128)(2,1)S(1)} %collective-permute-done.1.refs_2_), channel_id=1, source_target_pairs={{0,2},{1,3},{2,4},{3,5},{4,6},{5,7},{6,8},{7,9},{8,10},{9,11},{10,... | collective-permute-start | bytes 638984 | tf_op jit(solution)/shard_map/ppermute | solution.py:305
  101.8 13.0 %collective-permute-start.6 = (bf16[64,1664]{1,0:T(8,128)(2,1)S(1)}, bf16[64,1664]{1,0:T(8,128)(2,1)S(1)}, u32[]{:S(2)}, u32[]{:S(2)}) collective-permute-start(bf16[64,1664]{1,0:T(8,128)(2,1)S(1)} %collective-permute-done.5.refs_6_), channel_id=1, source_target_pairs={{0,14},{1,15},{2,0},{3,1},{4,2},{5,3},{6,4},{7,5},{8,6},{9,7},{10,... | collective-permute-start | bytes 638984 | tf_op jit(solution)/shard_map/ppermute | solution.py:307
  111.6 13.1 %collective-permute-start.3 = (bf16[64,1664]{1,0:T(8,128)(2,1)S(1)}, bf16[64,1664]{1,0:T(8,128)(2,1)S(1)}, u32[]{:S(2)}, u32[]{:S(2)}) collective-permute-start(bf16[64,1664]{1,0:T(8,128)(2,1)S(1)} %collective-permute-done.2.refs_3_), channel_id=1, source_target_pairs={{0,2},{1,3},{2,4},{3,5},{4,6},{5,7},{6,8},{7,9},{8,10},{9,11},{10,... | collective-permute-start | bytes 638984 | tf_op jit(solution)/shard_map/ppermute | solution.py:305
  126.1 11.6 %collective-permute-start.7 = (bf16[512,1664]{1,0:T(8,128)(2,1)}, bf16[512,1664]{1,0:T(8,128)(2,1)}, u32[]{:S(2)}, u32[]{:S(2)}) collective-permute-start(bf16[512,1664]{1,0:T(8,128)(2,1)} %stack_blocks.1.refs_2_), channel_id=1, source_target_pairs={{0,1},{1,0},{2,3},{3,2},{4,5},{5,4},{6,7},{7,6},{8,9},{9,8},{10,11... | collective-permute-start | bytes 5111816 | tf_op jit(solution)/shard_map/ppermute | solution.py:309
  141.6 1.1 copy-start.1
Sparse Core Ops, SparseCore 0:
  80.5 56.9 all-gather.1

commit v5 on v4

--- a/solution.py
+++ b/solution.py
@@ -277,7 +277,7 @@
     experts = lax.axis_size("tensor")
     rows, width = residual.shape
     slot_count = expert_hidden.shape[1] // experts
-    split = width * 5 // 8
+    split = width * 3 // 4
     expert_out = expert_project(expert_hidden[0], down_weight[0])
     returned = lax.all_to_all(
         expert_out.reshape(experts, slot_count, width),

time: 155 us -> 153 us (0.987)
  waiting for transfers between devices: 36.1 us -> 33.1 us
  local copies, waits for them, and re-layouts: 1.12 us -> 4 us
  starting transfers between devices: 47.7 us -> 45.9 us
    ppermute x4, waiting for transfers between devices: 19.8 us -> 12.9 us  [on_device(): ups.append(lax.ppermute(ups[-1], 'tensor', up))]
    all_gather x1, waiting for transfers between devices: 0.01 us -> 4.96 us  [on_device(): gathered = lax.all_gather(normed, 'tensor', axis=0, tiled=True)]
    unnamed x14 -> x18, local copies, waits for them, and re-layouts: 1.12 us -> 4 us
    ppermute x1, starting transfers between devices: 7.9 us -> 5.76 us  [on_device(): other = lax.ppermute(own, 'tensor', [(i, i ^ 1) for i in range(experts)])]
  transfers between devices with their start and end apart: 10 -> 10, of which waited for: 8 -> 9; matrix products, arithmetic and copies ran while one was open for 0% -> 0% of each run, Pallas kernels for 4% -> 3%
where the time goes in v5:
time: 153 us; the launch traced here: 152 us
  starting transfers between devices  45.9 us (30%)
  blocking collectives  38.5 us (25%)
  waiting for transfers between devices  33.1 us (22%)
  Pallas kernels  16.8 us (11%)
  between operations  14.2 us (9%)
  local copies, waits for them, and re-layouts  4 us (3%)
    psum x1, blocking collectives, on_device(): sums = lax.psum(sums, 'dp', axis_index_groups=lines)  31.9 us
    all_to_all x1, starting transfers between devices, on_device(): lax.all_to_all(expert_out.reshape(experts, slot_count, width), 'tensor',...  17.8 us
    ppermute x3, starting transfers between devices, on_device(): downs.append(lax.ppermute(downs[-1], 'tensor', down))  14.6 us
    ppermute x4, waiting for transfers between devices, on_device(): ups.append(lax.ppermute(ups[-1], 'tensor', up))  12.9 us
    all_to_all x1, waiting for transfers between devices, on_device(): lax.all_to_all(expert_out.reshape(experts, slot_count, width), 'tensor',...  10.2 us
    ppermute x4, starting transfers between devices, on_device(): ups.append(lax.ppermute(ups[-1], 'tensor', up))  7.65 us
    psum x1, blocking collectives, on_device(): sums = lax.psum((counts, shares), 'dp', axis_index_groups=cross)  6.6 us
    pallas_call x1, Pallas kernels, project(): pl.pallas_call(project_kernel, grid=(steps,), in_specs=[pl.BlockSpec((col...  5.88 us
  transfers between devices with their start and end apart: 10, of which 9 were waited for; matrix products, arithmetic and copies ran while one was open for 0% of the time, Pallas kernels for 3%

profile of v5, /device:TPU:1, one launch (start us, length us, event | category | flops | bytes accessed | tf_op | source)
XLA Modules:
  0.0 152.5 jit_solution(13463183100591995632)
XLA Ops:
  7.2 4.9 %expert_project.1 = bf16[256,4096]{1,0:T(8,128)(2,1)} custom-call(bf16[256,768]{1,0:T(8,128)(2,1)} %bitcast.22, bf16[768,4096]{1,0:T(8,128)(2,1)} %bitcast.20), custom_call_target="tpu_custom_call" | custom-call | flops 1610612736 | bytes 8781824 | tf_op jit(solution)/shard_map/expert_project/pallas_call | solution.py:32
  12.1 0.0 copy-start.4
  12.1 17.8 %all-to-all-start = ((bf16[16,16,4096]{2,1,0:T(8,128)(2,1)}), bf16[16,16,4096]{2,1,0:T(8,128)(2,1)S(1)}, u32[]{:S(2)}, u32[]{:S(2)}) async-start(bf16[16,16,4096]{2,1,0:T(8,128)(2,1)} %bitcast.19), calls=%async_computation | async-start | bytes 4194304 | tf_op jit(solution)/shard_map/all_to_all | solution.py:282
  29.9 0.0 all-gather.2.cloned.1.call-start
  30.0 0.2 pick_matrix.1
  30.2 6.6 %all-reduce.1 = (f32[1,16]{1,0:T(1,128)S(1)}, f32[1,16]{1,0:T(1,128)S(1)}) all-reduce(f32[1,16]{1,0:T(1,128)S(1)} %get-tuple-element.12, f32[1,16]{1,0:T(1,128)S(1)} %get-tuple-element.13), channel_id=1, replica_groups={{0,256,512,768},{16,272,528,784},{32,288,544,800},{48,304,560,816},{64,..., use_global_device_ids=true, to_apply=%region_0.0 | all-reduce | flops 32 | bytes 256 | tf_op jit(solution)/shard_map/psum | solution.py:294
  36.8 31.9 %all-reduce = (f32[1,16]{1,0:T(1,128)S(1)}, f32[1,16]{1,0:T(1,128)S(1)}) all-reduce(f32[1,16]{1,0:T(1,128)S(1)} %get-tuple-element.21, f32[1,16]{1,0:T(1,128)S(1)} %get-tuple-element.22), channel_id=1, replica_groups={{0,16,32,48,64,80,96,112,128,144,160,176,192,208,224,240},{256,272,288,..., use_global_device_ids=true, to_apply=%region_1.0 | all-reduce | flops 32 | bytes 256 | tf_op jit(solution)/shard_map/psum | solution.py:295
  68.8 10.2 %all-to-all-done = bf16[16,16,4096]{2,1,0:T(8,128)(2,1)S(1)} async-done(((bf16[16,16,4096]{2,1,0:T(8,128)(2,1)}), bf16[16,16,4096]{2,1,0:T(8,128)(2,1)S(1)}, u32[]{:S(2)}, u32[]{:S(2)}) %all-to-all-start) | async-done | bytes 2097184 | tf_op jit(solution)/shard_map/all_to_all | solution.py:282
  78.9 1.3 copy-done.1
  80.2 1.6 %copy-done.2 = bf16[16,16,4096]{2,1,0:T(8,128)(2,1)S(1)} copy-done((bf16[16,16,4096]{2,1,0:T(8,128)(2,1)S(1)}, bf16[16,16,4096]{2,1,0:T(8,128)(2,1)}, u32[]{:S(2)}) %copy-start.2) | copy-done | bytes 2097176
  81.8 1.4 combine_and_norm.1
  83.3 0.0 all-gather.2.cloned.1.call-update
  83.3 1.9 %collective-permute-start = (bf16[64,1152]{1,0:T(8,128)(2,1)S(1)}, bf16[64,1152]{1,0:T(8,128)(2,1)S(1)}, u32[]{:S(2)}, u32[]{:S(2)}) collective-permute-start(bf16[64,1152]{1,0:T(8,128)(2,1)S(1)} %get-tuple-element.16.refs_0_), channel_id=1, source_target_pairs={{0,2},{1,3},{2,4},{3,5},{4,6},{5,7},{6,8},{7,9},{8,10},{9,11},{10,... | collective-permute-start | bytes 442376 | tf_op jit(solution)/shard_map/ppermute | solution.py:305
  85.2 4.6 %collective-permute-start.4 = (bf16[64,1152]{1,0:T(8,128)(2,1)S(1)}, bf16[64,1152]{1,0:T(8,128)(2,1)S(1)}, u32[]{:S(2)}, u32[]{:S(2)}) collective-permute-start(bf16[64,1152]{1,0:T(8,128)(2,1)S(1)} %get-tuple-element.16.refs_0_), channel_id=1, source_target_pairs={{0,14},{1,15},{2,0},{3,1},{4,2},{5,3},{6,4},{7,5},{8,6},{9,7},{10,... | collective-permute-start | bytes 442376 | tf_op jit(solution)/shard_map/ppermute | solution.py:307
  89.8 1.6 %collective-permute-done.refs_1_ = bf16[64,1152]{1,0:T(8,128)(2,1)S(1)} collective-permute-done((bf16[64,1152]{1,0:T(8,128)(2,1)S(1)}, bf16[64,1152]{1,0:T(8,128)(2,1)S(1)}, u32[]{:S(2)}, u32[]{:S(2)}) %collective-permute-start) | collective-permute-done | bytes 147488 | tf_op jit(solution)/shard_map/ppermute | solution.py:305
  91.4 1.9 %collective-permute-start.1 = (bf16[64,1152]{1,0:T(8,128)(2,1)S(1)}, bf16[64,1152]{1,0:T(8,128)(2,1)S(1)}, u32[]{:S(2)}, u32[]{:S(2)}) collective-permute-start(bf16[64,1152]{1,0:T(8,128)(2,1)S(1)} %collective-permute-done.refs_1_), channel_id=1, source_target_pairs={{0,2},{1,3},{2,4},{3,5},{4,6},{5,7},{6,8},{7,9},{8,10},{9,11},{10,... | collective-permute-start | bytes 442376 | tf_op jit(solution)/shard_map/ppermute | solution.py:305
  93.3 4.6 %collective-permute-start.5 = (bf16[64,1152]{1,0:T(8,128)(2,1)S(1)}, bf16[64,1152]{1,0:T(8,128)(2,1)S(1)}, u32[]{:S(2)}, u32[]{:S(2)}) collective-permute-start(bf16[64,1152]{1,0:T(8,128)(2,1)S(1)} %collective-permute-done.4.refs_7_), channel_id=1, source_target_pairs={{0,14},{1,15},{2,0},{3,1},{4,2},{5,3},{6,4},{7,5},{8,6},{9,7},{10,... | collective-permute-start | bytes 442376 | tf_op jit(solution)/shard_map/ppermute | solution.py:307
  97.9 0.6 collective-permute-done.1.refs_2_
  98.5 1.9 %collective-permute-start.2 = (bf16[64,1152]{1,0:T(8,128)(2,1)S(1)}, bf16[64,1152]{1,0:T(8,128)(2,1)S(1)}, u32[]{:S(2)}, u32[]{:S(2)}) collective-permute-start(bf16[64,1152]{1,0:T(8,128)(2,1)S(1)} %collective-permute-done.1.refs_2_), channel_id=1, source_target_pairs={{0,2},{1,3},{2,4},{3,5},{4,6},{5,7},{6,8},{7,9},{8,10},{9,11},{10,... | collective-permute-start | bytes 442376 | tf_op jit(solution)/shard_map/ppermute | solution.py:305
  100.4 1.5 collective-permute-done.5.refs_6_
  101.9 5.5 %collective-permute-start.6 = (bf16[64,1152]{1,0:T(8,128)(2,1)S(1)}, bf16[64,1152]{1,0:T(8,128)(2,1)S(1)}, u32[]{:S(2)}, u32[]{:S(2)}) collective-permute-start(bf16[64,1152]{1,0:T(8,128)(2,1)S(1)} %collective-permute-done.5.refs_6_), channel_id=1, source_target_pairs={{0,14},{1,15},{2,0},{3,1},{4,2},{5,3},{6,4},{7,5},{8,6},{9,7},{10,... | collective-permute-start | bytes 442376 | tf_op jit(solution)/shard_map/ppermute | solution.py:307
  107.4 2.4 %collective-permute-done.2.refs_3_ = bf16[64,1152]{1,0:T(8,128)(2,1)S(1)} collective-permute-done((bf16[64,1152]{1,0:T(8,128)(2,1)S(1)}, bf16[64,1152]{1,0:T(8,128)(2,1)S(1)}, u32[]{:S(2)}, u32[]{:S(2)}) %collective-permute-start.2) | collective-permute-done | bytes 147488 | tf_op jit(solution)/shard_map/ppermute | solution.py:305
  109.8 1.9 %collective-permute-start.3 = (bf16[64,1152]{1,0:T(8,128)(2,1)S(1)}, bf16[64,1152]{1,0:T(8,128)(2,1)S(1)}, u32[]{:S(2)}, u32[]{:S(2)}) collective-permute-start(bf16[64,1152]{1,0:T(8,128)(2,1)S(1)} %collective-permute-done.2.refs_3_), channel_id=1, source_target_pairs={{0,2},{1,3},{2,4},{3,5},{4,6},{5,7},{6,8},{7,9},{8,10},{9,11},{10,... | collective-permute-start | bytes 442376 | tf_op jit(solution)/shard_map/ppermute | solution.py:305
  111.7 0.7 collective-permute-done.6.refs_5_
  112.4 8.4 %collective-permute-done.3.refs_4_ = bf16[64,1152]{1,0:T(8,128)(2,1)S(1)} collective-permute-done((bf16[64,1152]{1,0:T(8,128)(2,1)S(1)}, bf16[64,1152]{1,0:T(8,128)(2,1)S(1)}, u32[]{:S(2)}, u32[]{:S(2)}) %collective-permute-start.3) | collective-permute-done | bytes 147488 | tf_op jit(solution)/shard_map/ppermute | solution.py:305
  120.8 1.1 stack_blocks.1.refs_2_
  121.9 5.8 %collective-permute-start.7 = (bf16[512,1152]{1,0:T(8,128)(2,1)}, bf16[512,1152]{1,0:T(8,128)(2,1)}, u32[]{:S(2)}, u32[]{:S(2)}) collective-permute-start(bf16[512,1152]{1,0:T(8,128)(2,1)} %stack_blocks.1.refs_2_), channel_id=1, source_target_pairs={{0,1},{1,0},{2,3},{3,2},{4,5},{5,4},{6,7},{7,6},{8,9},{9,8},{10,11... | collective-permute-start | bytes 3538952 | tf_op jit(solution)/shard_map/ppermute | solution.py:309
  127.6 2.9 %collective-permute-done.7.refs_3_ = bf16[512,1152]{1,0:T(8,128)(2,1)} collective-permute-done((bf16[512,1152]{1,0:T(8,128)(2,1)}, bf16[512,1152]{1,0:T(8,128)(2,1)}, u32[]{:S(2)}, u32[]{:S(2)}) %collective-permute-start.7) | collective-permute-done | bytes 1179680 | tf_op jit(solution)/shard_map/ppermute | solution.py:309
  130.5 3.2 %ring_project.1 = (f32[320,1024]{1,0:T(8,128)S(1)}, f32[1,1]{1,0:T(1,128)}) custom-call(s32[1]{0:T(128)} %bitcast.9.refs_0_, bf16[320,4096]{1,0:T(8,128)(2,1)S(1)} %bitcast.13, bf16[512,1152]{1,0:T(8,128)(2,1)} %stack_blocks.1.refs_2_, bf16[512,1152]{1,0:T(8,128)(2,1)} %collective-permute-done.7.refs_3_), custom_call_target="tpu_custom_call" | custom-call | flops 671088640 | bytes 6029312 | tf_op jit(solution)/shard_map/ring_project/pallas_call | solution.py:221
  133.7 1.1 copy-done.3
  134.8 5.0 %all-gather.2.cloned.1.call-done.rows_ref = bf16[1024,3072]{1,0:T(8,128)(2,1)} async-done(((bf16[64,3072]{1,0:T(8,128)(2,1)}), bf16[1024,3072]{1,0:T(8,128)(2,1)}) %all-gather.2.cloned.1.call-update) | async-done | bytes 6291472 | tf_op jit(solution)/shard_map/all_gather | solution.py:299
  139.8 5.9 %qkv_project.1 = bf16[320,1024]{1,0:T(8,128)(2,1)} custom-call(bf16[320,4096]{1,0:T(8,128)(2,1)} %bitcast.12, bf16[1024,3072]{1,0:T(8,128)(2,1)} %all-gather.2.cloned.1.call-done.rows_ref, f32[320,1024]{1,0:T(8,128)} %copy-done.3), custom_call_target="tpu_custom_call" | custom-call | flops 2013265920 | bytes 10223616 | tf_op jit(solution)/shard_map/qkv_project/pallas_call | solution.py:254
  (15 shorter events, 0.0 us)
Async XLA Ops:
  12.1 17.9 %copy-start.6 = (f32[64,16]{0,1:T(8,128)S(1)}, f32[64,16]{0,1:T(8,128)}, u32[]{:S(2)}) copy-start(f32[64,16]{0,1:T(8,128)} %param.13) | copy-start | bytes 12292
  12.1 17.9 %copy-start.7 = (s32[64,2]{0,1:T(2,128)S(1)}, s32[64,2]{0,1:T(2,128)}, u32[]{:S(2)}) copy-start(s32[64,2]{0,1:T(2,128)} %param.12) | copy-start | bytes 1540
  12.1 17.9 %copy-start.8 = (f32[64,2]{0,1:T(2,128)S(1)}, f32[64,2]{0,1:T(2,128)}, u32[]{:S(2)}) copy-start(f32[64,2]{0,1:T(2,128)} %param.11) | copy-start | bytes 1540
  12.1 68.1 %copy-start.4 = (bf16[64,4096]{1,0:T(8,128)(2,1)S(1)}, bf16[64,4096]{1,0:T(8,128)(2,1)}, u32[]{:S(2)}) copy-start(bf16[64,4096]{1,0:T(8,128)(2,1)} %residual_ref.1) | copy-start | bytes 1572868
  12.1 68.1 %copy-start.5 = (f32[4096]{0:T(1024)S(1)}, f32[4096]{0:T(1024)}, u32[]{:S(2)}) copy-start(f32[4096]{0:T(1024)} %param.14) | copy-start | bytes 49156
  12.1 66.8 %all-to-all-start = ((bf16[16,16,4096]{2,1,0:T(8,128)(2,1)}), bf16[16,16,4096]{2,1,0:T(8,128)(2,1)S(1)}, u32[]{:S(2)}, u32[]{:S(2)}) async-start(bf16[16,16,4096]{2,1,0:T(8,128)(2,1)} %bitcast.19), calls=%async_computation | async-start | bytes 4194304 | tf_op jit(solution)/shard_map/all_to_all | solution.py:282
  29.9 109.8 %all-gather.2.cloned.1.call-start = ((), (), s32[]{:S(2)}) async-start(), calls=%async_computation.1 | async-start | bytes 6684672 | tf_op jit(solution)/shard_map/all_gather | solution.py:299
  78.9 1.3 copy-start.1
  80.2 1.6 %copy-start.2 = (bf16[16,16,4096]{2,1,0:T(8,128)(2,1)S(1)}, bf16[16,16,4096]{2,1,0:T(8,128)(2,1)}, u32[]{:S(2)}) copy-start(bf16[16,16,4096]{2,1,0:T(8,128)(2,1)} %copy-done.1) | copy-start | bytes 6291460
  81.8 48.7 %copy-start = (bf16[4096,320]{0,1:T(8,128)(2,1)S(1)}, bf16[4096,320]{0,1:T(8,128)(2,1)}, u32[]{:S(2)}) copy-start(bf16[4096,320]{0,1:T(8,128)(2,1)} %param.15) | copy-start | bytes 7864324
  83.3 8.1 %collective-permute-start = (bf16[64,1152]{1,0:T(8,128)(2,1)S(1)}, bf16[64,1152]{1,0:T(8,128)(2,1)S(1)}, u32[]{:S(2)}, u32[]{:S(2)}) collective-permute-start(bf16[64,1152]{1,0:T(8,128)(2,1)S(1)} %get-tuple-element.16.refs_0_), channel_id=1, source_target_pairs={{0,2},{1,3},{2,4},{3,5},{4,6},{5,7},{6,8},{7,9},{8,10},{9,11},{10,... | collective-permute-start | bytes 442376 | tf_op jit(solution)/shard_map/ppermute | solution.py:305
  85.2 8.1 %collective-permute-start.4 = (bf16[64,1152]{1,0:T(8,128)(2,1)S(1)}, bf16[64,1152]{1,0:T(8,128)(2,1)S(1)}, u32[]{:S(2)}, u32[]{:S(2)}) collective-permute-start(bf16[64,1152]{1,0:T(8,128)(2,1)S(1)} %get-tuple-element.16.refs_0_), channel_id=1, source_target_pairs={{0,14},{1,15},{2,0},{3,1},{4,2},{5,3},{6,4},{7,5},{8,6},{9,7},{10,... | collective-permute-start | bytes 442376 | tf_op jit(solution)/shard_map/ppermute | solution.py:307
  91.4 7.1 %collective-permute-start.1 = (bf16[64,1152]{1,0:T(8,128)(2,1)S(1)}, bf16[64,1152]{1,0:T(8,128)(2,1)S(1)}, u32[]{:S(2)}, u32[]{:S(2)}) collective-permute-start(bf16[64,1152]{1,0:T(8,128)(2,1)S(1)} %collective-permute-done.refs_1_), channel_id=1, source_target_pairs={{0,2},{1,3},{2,4},{3,5},{4,6},{5,7},{6,8},{7,9},{8,10},{9,11},{10,... | collective-permute-start | bytes 442376 | tf_op jit(solution)/shard_map/ppermute | solution.py:305
  93.3 8.5 %collective-permute-start.5 = (bf16[64,1152]{1,0:T(8,128)(2,1)S(1)}, bf16[64,1152]{1,0:T(8,128)(2,1)S(1)}, u32[]{:S(2)}, u32[]{:S(2)}) collective-permute-start(bf16[64,1152]{1,0:T(8,128)(2,1)S(1)} %collective-permute-done.4.refs_7_), channel_id=1, source_target_pairs={{0,14},{1,15},{2,0},{3,1},{4,2},{5,3},{6,4},{7,5},{8,6},{9,7},{10,... | collective-permute-start | bytes 442376 | tf_op jit(solution)/shard_map/ppermute | solution.py:307
  98.5 11.2 %collective-permute-start.2 = (bf16[64,1152]{1,0:T(8,128)(2,1)S(1)}, bf16[64,1152]{1,0:T(8,128)(2,1)S(1)}, u32[]{:S(2)}, u32[]{:S(2)}) collective-permute-start(bf16[64,1152]{1,0:T(8,128)(2,1)S(1)} %collective-permute-done.1.refs_2_), channel_id=1, source_target_pairs={{0,2},{1,3},{2,4},{3,5},{4,6},{5,7},{6,8},{7,9},{8,10},{9,11},{10,... | collective-permute-start | bytes 442376 | tf_op jit(solution)/shard_map/ppermute | solution.py:305
  101.9 10.5 %collective-permute-start.6 = (bf16[64,1152]{1,0:T(8,128)(2,1)S(1)}, bf16[64,1152]{1,0:T(8,128)(2,1)S(1)}, u32[]{:S(2)}, u32[]{:S(2)}) collective-permute-start(bf16[64,1152]{1,0:T(8,128)(2,1)S(1)} %collective-permute-done.5.refs_6_), channel_id=1, source_target_pairs={{0,14},{1,15},{2,0},{3,1},{4,2},{5,3},{6,4},{7,5},{8,6},{9,7},{10,... | collective-permute-start | bytes 442376 | tf_op jit(solution)/shard_map/ppermute | solution.py:307
  109.8 11.0 %collective-permute-start.3 = (bf16[64,1152]{1,0:T(8,128)(2,1)S(1)}, bf16[64,1152]{1,0:T(8,128)(2,1)S(1)}, u32[]{:S(2)}, u32[]{:S(2)}) collective-permute-start(bf16[64,1152]{1,0:T(8,128)(2,1)S(1)} %collective-permute-done.2.refs_3_), channel_id=1, source_target_pairs={{0,2},{1,3},{2,4},{3,5},{4,6},{5,7},{6,8},{7,9},{8,10},{9,11},{10,... | collective-permute-start | bytes 442376 | tf_op jit(solution)/shard_map/ppermute | solution.py:305
  121.9 8.7 %collective-permute-start.7 = (bf16[512,1152]{1,0:T(8,128)(2,1)}, bf16[512,1152]{1,0:T(8,128)(2,1)}, u32[]{:S(2)}, u32[]{:S(2)}) collective-permute-start(bf16[512,1152]{1,0:T(8,128)(2,1)} %stack_blocks.1.refs_2_), channel_id=1, source_target_pairs={{0,1},{1,0},{2,3},{3,2},{4,5},{5,4},{6,7},{7,6},{8,9},{9,8},{10,11... | collective-permute-start | bytes 3538952 | tf_op jit(solution)/shard_map/ppermute | solution.py:309
  133.7 1.1 copy-start.3
Sparse Core Ops, SparseCore 0:
  83.4 56.2 all-gather.1
